TPU v7x, 32 devices: a whole 2x2x4 slice. The times are simulated.
32 devices in a mesh: dp: 8 (over z, x), seq: 4 (over y, core).
Axes of the slice: x: 2, y: 2, z: 4, core: 2. Of those that a mesh axis runs over, the one named last changes fastest.
Arguments:
- tokens: bfloat16 [32, 1024, 768], P('dp', 'seq'), may hold values from -6 to 6
- cotangent: bfloat16 [32, 1024, 768], P('dp', 'seq'), may hold values from -6 to 6
- lengths: int32 [32], P('dp'), may hold values from 1 to 1024, as said below
- qkv_weight: float32 [768, 2304], P('dp'), may hold values from -0.21875 to 0.21875
- qkv_first: float32 [768, 2304], P('dp'), may hold values from -0.00390625 to 0.00390625
- qkv_second: float32 [768, 2304], P('dp'), may hold values from 5.4253474e-07 to 2.170139e-06
- qkv_average: float32 [768, 2304], P('dp'), may hold values from -0.21875 to 0.21875
- proj_weight: float32 [768, 768], P('dp'), may hold values from -1.75 to 1.75
- proj_first: float32 [768, 768], P('dp'), may hold values from -0.00048828125 to 0.00048828125
- proj_second: float32 [768, 768], P('dp'), may hold values from 6.781684e-09 to 2.7126736e-08
- proj_average: float32 [768, 768], P('dp'), may hold values from -1.75 to 1.75
- inner_weight: float32 [768, 3072], P('dp'), may hold values from -0.21875 to 0.21875
- inner_first: float32 [768, 3072], P('dp'), may hold values from -0.0004272461 to 0.0004272461
- inner_second: float32 [768, 3072], P('dp'), may hold values from 5.086263e-09 to 2.0345052e-08
- inner_average: float32 [768, 3072], P('dp'), may hold values from -0.21875 to 0.21875
- outer_weight: float32 [3072, 768], P('dp'), may hold values from -0.109375 to 0.109375
- outer_first: float32 [3072, 768], P('dp'), may hold values from -0.0007324219 to 0.0007324219
- outer_second: float32 [3072, 768], P('dp'), may hold values from 1.2715658e-08 to 5.086263e-08
- outer_average: float32 [3072, 768], P('dp'), may hold values from -0.109375 to 0.109375
- gains: float32 [2, 768], P(None, 'dp'), may hold values from 0.3 to 2.4
- gain_first: float32 [2, 768], P(None, 'dp'), may hold values from -0.009765625 to 0.009765625
- gain_second: float32 [2, 768], P(None, 'dp'), may hold values from 2.2605614e-06 to 9.042245e-06
- gain_average: float32 [2, 768], P(None, 'dp'), may hold values from 0.1 to 1.9
- mixes: float32 [2, 12, 12], replicated, may hold values from -0.9 to 1.3
- mix_first: float32 [2, 12, 12], replicated, may hold values from -0.01953125 to 0.01953125
- mix_second: float32 [2, 12, 12], replicated, may hold values from 9.042245e-06 to 3.616898e-05
- mix_average: float32 [2, 12, 12], replicated, may hold values from -0.4 to 1.2
Outputs:
- output: bfloat16 [32, 1024, 768], P('dp', 'seq')
- grad_tokens: float32 [32, 1024, 768], P('dp', 'seq')
- grad_norm: float32 [], replicated
- next_qkv_first: float32 [768, 2304], P('dp')
- next_qkv_second: float32 [768, 2304], P('dp')
- next_qkv_weight: float32 [768, 2304], P('dp')
- next_qkv_average: float32 [768, 2304], P('dp')
- next_proj_first: float32 [768, 768], P('dp')
- next_proj_second: float32 [768, 768], P('dp')
- next_proj_weight: float32 [768, 768], P('dp')
- next_proj_average: float32 [768, 768], P('dp')
- next_inner_first: float32 [768, 3072], P('dp')
- next_inner_second: float32 [768, 3072], P('dp')
- next_inner_weight: float32 [768, 3072], P('dp')
- next_inner_average: float32 [768, 3072], P('dp')
- next_outer_first: float32 [3072, 768], P('dp')
- next_outer_second: float32 [3072, 768], P('dp')
- next_outer_weight: float32 [3072, 768], P('dp')
- next_outer_average: float32 [3072, 768], P('dp')
- next_gain_first: float32 [2, 768], P(None, 'dp')
- next_gain_second: float32 [2, 768], P(None, 'dp')
- next_gains: float32 [2, 768], P(None, 'dp')
- next_gain_average: float32 [2, 768], P(None, 'dp')
- next_mix_first: float32 [2, 12, 12], replicated
- next_mix_second: float32 [2, 12, 12], replicated
- next_mixes: float32 [2, 12, 12], replicated
- next_mix_average: float32 [2, 12, 12], replicated
- clipped_gain_grad: float32 [2, 768], P(None, 'dp')
Inputs may be any that keep to these rules, and one draw needn't show every extreme that they name: `lengths`: in each aligned block of 4 sequences (one index of dp) at least one sequence has length 1024.
All inputs are finite; a program needn't handle non-finite values.
Results may differ from a plain program's by a relative error of at most 0.014.
The roundings to bfloat16 on the way count: a program that leaves them out, or rounds other values in their place, can miss the bound.
Values may be sent and summed in bfloat16 or wider, within the bound.
No kernel may reach another device: no remote copies, remote signals or barrier semaphores. Data moves between devices by JAX's collectives and lax.ppermute only.
A program may use at most 384 MiB of HBM per device.

v0:
```python
from functools import partial
import math

import jax
import jax.numpy as jnp
from jax import lax
from jax.experimental import pallas as pl
from jax.experimental.pallas import tpu as pltpu
from jax.sharding import PartitionSpec as P

STEP = 10

NORM_EPS = 1e-06
BETA = 0.5
ADAM_EPS = 1e-08
DECAY = 0.01
EMA_KEEP = 0.8
CLIP = 1.0

BF = jnp.bfloat16
F32 = jnp.float32
ROWS = 128
KEYS = 256
GROUP = 16
LANES = 128
FLOPS = (60 * 10**9, 1)
SIDE = {1: 8, 2: 8, 3: 8, 4: 8}
SIDE_BACK = {1: 4, 2: 4, 3: 2, 4: 2}
NT = (((1,), (1,)), ((), ()))
NN = (((1,), (0,)), ((), ()))
TN = (((0,), (0,)), ((), ()))


def dot(left, right, dims=NN):
    return lax.dot_general(left, right, dims, preferred_element_type=F32)


def inverse_rms(values):
    return lax.rsqrt(jnp.mean(values * values, axis=-1, keepdims=True) + NORM_EPS)


def rms_backward(scale_inv, normed, grad_normed):
    return scale_inv * (
        grad_normed - normed * jnp.mean(normed * grad_normed, axis=-1, keepdims=True)
    )


def adamw(weight, first, second, average, grad, rate):
    first_new = BETA * first + (1.0 - BETA) * grad
    second_new = BETA * second + (1.0 - BETA) * grad * grad
    fix = 1.0 - BETA**STEP
    weight_new = weight - rate * (
        first_new / fix / (jnp.sqrt(second_new / fix) + ADAM_EPS) + DECAY * weight
    )
    average_new = EMA_KEEP * average + (1.0 - EMA_KEEP) * weight_new
    return (first_new, second_new, weight_new, average_new)


def swap(value, axis, mask):
    size = lax.axis_size(axis)
    return lax.ppermute(value, axis, [(i, i ^ mask) for i in range(size)])


def digits_of(size):
    found = []
    stride = 1
    while stride < size:
        radix = 2 if stride == 1 or size // stride < 4 else 4
        found.append((stride, radix))
        stride *= radix
    return found


def gather_steps(size):
    steps = []
    while size > 1:
        size //= 2
        steps.append(size)
    return steps


def own_order(shards, axis):
    size = shards.shape[0]
    order = jnp.bitwise_xor(jnp.arange(size, dtype=jnp.int32), lax.axis_index(axis))
    return shards.at[order].get(mode="promise_in_bounds")


def join_pieces(pieces, axis):
    place = {}
    for _, offs in pieces:
        for off in offs:
            place[off] = len(place)
    spots = jnp.array([place[off] for off in range(len(place))], jnp.int32)
    order = jnp.bitwise_xor(jnp.arange(len(place), dtype=jnp.int32), lax.axis_index(axis))
    whole = jnp.concatenate([piece for piece, _ in pieces])
    return whole.at[spots.at[order].get(mode="promise_in_bounds")].get(mode="promise_in_bounds")


def split_blocks(blocks, axis, digits, digit):
    stride, radix = digit
    place = digits.index(digit)
    mine = (lax.axis_index(axis) // stride) % radix
    parts = [
        lax.dynamic_index_in_dim(blocks, jnp.bitwise_xor(mine, k), place, False)
        for k in range(radix)
    ]
    return parts, [d for d in digits if d != digit]


def join_blocks(parts, axis, digit, *first):
    stride, radix = digit
    got = tuple(swap(parts[k], axis, k * stride) for k in range(1, radix))
    if first:
        got = after(got, *first)
    total = parts[0].astype(F32)
    for part in got:
        total = total + part.astype(F32)
    return total


def sum_everywhere(value, axis):
    size = lax.axis_size(axis)
    stride = 1
    while stride < size:
        radix = min(8, size // stride)
        parts = [value] + [swap(value, axis, k * stride) for k in range(1, radix)]
        while len(parts) > 1:
            parts = [parts[i] + parts[i + 1] for i in range(0, len(parts), 2)]
        value = parts[0]
        stride *= radix
    return value


def after(value, *first):
    return lax.optimization_barrier((value,) + first)[0]


def spread_kernel(mixes, pre, post, pre_back, post_back):
    heads = mixes.shape[1]
    tall = heads * GROUP
    wide = (lax.broadcasted_iota(jnp.int32, (tall, heads), 0) // GROUP) == (
        lax.broadcasted_iota(jnp.int32, (tall, heads), 1)
    )
    wide = wide.astype(F32)
    row = lax.broadcasted_iota(jnp.int32, (tall, tall), 0)
    col = lax.broadcasted_iota(jnp.int32, (tall, tall), 1)
    same = row % GROUP == col % GROUP

    def exact(left, right, dims):
        return lax.dot_general(
            left, right, dims, precision=lax.Precision.HIGHEST, preferred_element_type=F32
        )

    for which, (turned, straight) in enumerate(((pre, pre_back), (post, post_back))):
        matrix = mixes[which]
        for out, dims in ((straight, NN), (turned, NT)):
            tallest = exact(wide, matrix, dims)
            full = jnp.where(same, exact(tallest, wide, NT), 0.0)
            high = full.astype(BF)
            out[:tall, :] = high
            out[tall:, :] = (full - high.astype(F32)).astype(BF)


def spread(mixes):
    tall = mixes.shape[1] * GROUP
    return pl.pallas_call(
        spread_kernel,
        out_shape=[jax.ShapeDtypeStruct((2 * tall, tall), BF)] * 4,
        name="spread",
    )(mixes)


def two_heads(rows, first, second):
    return jnp.concatenate([rows * first, rows * second], 0)


def mix(matrix, values):
    out = dot(matrix, values)
    half = matrix.shape[0] // 2
    return out[:half] + out[half:]


def head_masks(scaling):
    lane = lax.broadcasted_iota(jnp.int32, (1, LANES), 1)
    low = lane < LANES // 2
    return low, jnp.where(low, scaling, 0.0).astype(BF), jnp.where(low, 0.0, scaling).astype(BF)


def fill_sequence(meta, sources, qkv, sems):
    copies = []
    for d, source in enumerate(sources):
        start = pl.multiple_of(jnp.bitwise_xor(meta[1], d) * KEYS, KEYS)
        copies.append(pltpu.make_async_copy(source, qkv.at[pl.ds(start, KEYS)], sems.at[d]))
    for copy in copies:
        copy.start()
    for copy in copies:
        copy.wait()


def forward_kernel(meta, *refs):
    sources, (pre, post, attended, probs, weights, qkv, held, sems) = refs[:4], refs[4:]
    heads = probs.shape[0]
    width = attended.shape[1]
    pairs = heads // 2
    tall = heads * GROUP
    step = pl.program_id(0)
    pl.when(step == 0)(partial(fill_sequence, meta, sources, qkv, sems))
    length = meta[0]
    row0 = pl.multiple_of(step * KEYS + meta[2] * ROWS, ROWS)
    chunks = (jnp.minimum(row0 + ROWS, length) + KEYS - 1) // KEYS
    low, first_s, second_s = head_masks(1.0 / math.sqrt(width // heads))

    def score(kc, carry):
        k0 = pl.multiple_of(kc * KEYS, KEYS)
        for p in range(pairs):
            at = p * LANES
            queries = two_heads(qkv[pl.ds(row0, ROWS), at : at + LANES], first_s, second_s)
            keys = qkv[pl.ds(k0, KEYS), width + at : width + at + LANES]
            scores = dot(queries, keys, NT).astype(BF)
            weights[2 * p : 2 * p + 2, :, pl.ds(k0, KEYS)] = scores.reshape(2, ROWS, KEYS)
        return carry

    lax.fori_loop(0, chunks, score, 0)

    def group(n, batch, carry):
        side = SIDE[n]
        rows = [
            pl.ds(pl.multiple_of((batch * side + u) * GROUP, GROUP), GROUP) for u in range(side)
        ]
        col_at = lax.broadcasted_iota(jnp.int32, (GROUP, KEYS), 1)
        row_at = lax.broadcasted_iota(jnp.int32, (GROUP, KEYS), 0)
        peak = [None] * side
        total = [None] * side
        for kc in range(n):
            cols = slice(kc * KEYS, (kc + 1) * KEYS)
            for u in range(side):
                mixed = mix(pre[...], weights[:, rows[u], cols].reshape(tall, KEYS))
                key_pos = col_at + kc * KEYS
                query_pos = row0 + (batch * side + u) * GROUP + row_at
                allowed = (key_pos <= query_pos) & (key_pos < length)
                mixed = jnp.where(allowed[None], mixed.reshape(heads, GROUP, KEYS), -1e30)
                mixed = mixed.reshape(tall, KEYS)
                held[u, :, cols] = mixed
                part = jnp.maximum(mixed[:, :LANES], mixed[:, LANES:])
                peak[u] = part if kc == 0 else jnp.maximum(peak[u], part)
        top = [jnp.max(peak[u], axis=1, keepdims=True) for u in range(side)]
        for kc in range(n):
            cols = slice(kc * KEYS, (kc + 1) * KEYS)
            for u in range(side):
                shifted = jnp.exp(held[u, :, cols] - top[u])
                held[u, :, cols] = shifted
                part = shifted[:, :LANES] + shifted[:, LANES:]
                total[u] = part if kc == 0 else total[u] + part
        inverse = [1.0 / jnp.sum(total[u], axis=1, keepdims=True) for u in range(side)]
        for kc in range(n):
            cols = slice(kc * KEYS, (kc + 1) * KEYS)
            for u in range(side):
                low_probs = (held[u, :, cols] * inverse[u]).astype(BF)
                probs[:, rows[u], cols] = low_probs.reshape(heads, GROUP, KEYS)
                mixed = mix(post[...], low_probs).astype(BF)
                weights[:, rows[u], cols] = mixed.reshape(heads, GROUP, KEYS)
        return carry

    def rest(n):
        lax.fori_loop(0, ROWS // GROUP // SIDE[n], partial(group, n), 0)
        for p in range(pairs):
            at = p * LANES
            pair = weights[2 * p : 2 * p + 2, :, : n * KEYS].reshape(2 * ROWS, n * KEYS)
            out = dot(pair, qkv[: n * KEYS, 2 * width + at : 2 * width + at + LANES])
            attended[:, at : at + LANES] = jnp.where(low, out[:ROWS], out[ROWS:]).astype(BF)

    for n in range(1, probs.shape[2] // KEYS + 1):
        pl.when(chunks == n)(partial(rest, n))


def backward_kernel(meta, *refs):
    sources, refs = refs[:4], refs[4:]
    grad_rows, pre, post, probs, weights, stay, away, grad_pre, grad_post = refs[:9]
    qkv, scores, grads, held, grad_qkv, sum_pre, sum_post, sems = refs[9:]
    heads = probs.shape[0]
    width = grad_rows.shape[1]
    pairs = heads // 2
    tall = heads * GROUP
    step = pl.program_id(0)
    me = meta[1]

    @pl.when(step == 0)
    def _():
        grad_qkv[...] = jnp.zeros_like(grad_qkv)
        sum_pre[...] = jnp.zeros_like(sum_pre)
        sum_post[...] = jnp.zeros_like(sum_post)
        fill_sequence(meta, sources, qkv, sems)

    length = meta[0]
    row0 = pl.multiple_of(step * KEYS + meta[2] * ROWS, ROWS)
    chunks = (jnp.minimum(row0 + ROWS, length) + KEYS - 1) // KEYS
    chunks = jnp.where(row0 < length, chunks, 0)
    scaling = 1.0 / math.sqrt(width // heads)
    low, first_s, second_s = head_masks(scaling)
    low, first_one, second_one = head_masks(1.0)
    lanes = pl.ds(pl.multiple_of(meta[2] * ROWS, ROWS), ROWS)

    def slot_of(home):
        d = jnp.bitwise_xor(me, home)
        return 2 * jnp.bitwise_and(d, 1) + d // 2


    def score(kc, carry):
        k0 = pl.multiple_of(kc * KEYS, KEYS)
        for p in range(pairs):
            at = p * LANES
            queries = two_heads(qkv[pl.ds(row0, ROWS), at : at + LANES], first_s, second_s)
            grad = two_heads(grad_rows[:, at : at + LANES], first_one, second_one)
            keys = qkv[pl.ds(k0, KEYS), width + at : width + at + LANES]
            values = qkv[pl.ds(k0, KEYS), 2 * width + at : 2 * width + at + LANES]
            both = slice(2 * p, 2 * p + 2)
            cols = pl.ds(k0, KEYS)
            scores[both, :, cols] = dot(queries, keys, NT).astype(BF).reshape(2, ROWS, KEYS)
            grads[both, :, cols] = dot(grad, values, NT).astype(BF).reshape(2, ROWS, KEYS)
        return carry

    lax.fori_loop(0, chunks, score, 0)

    def group(n, batch, carry):
        side = SIDE_BACK[n]
        rows = [
            pl.ds(pl.multiple_of((batch * side + u) * GROUP, GROUP), GROUP) for u in range(side)
        ]
        span = slice(0, n * KEYS)
        total = [None] * side
        for kc in range(n):
            cols = slice(kc * KEYS, (kc + 1) * KEYS)
            for u in range(side):
                grad_probs = mix(post[...], grads[:, rows[u], cols].reshape(tall, KEYS))
                held[u, :, cols] = grad_probs
                term = probs[:, rows[u], cols].reshape(tall, KEYS).astype(F32) * grad_probs
                part = term[:, :LANES] + term[:, LANES:]
                total[u] = part if kc == 0 else total[u] + part
        added = None
        for u in range(side):
            left = probs[:, rows[u], span].reshape(tall, n * KEYS)
            term = dot(left, grads[:, rows[u], span].reshape(tall, n * KEYS), NT)
            added = term if u == 0 else added + term
        sum_post[...] += added
        delta = [jnp.sum(total[u], axis=1, keepdims=True) for u in range(side)]
        mixed = [[] for _ in range(side)]
        for kc in range(n):
            cols = slice(kc * KEYS, (kc + 1) * KEYS)
            for u in range(side):
                prob = probs[:, rows[u], cols].reshape(tall, KEYS).astype(F32)
                grad_mixed = (prob * (held[u, :, cols] - delta[u])).astype(BF)
                mixed[u].append(grad_mixed)
                back = mix(pre[...], grad_mixed).astype(BF)
                grads[:, rows[u], cols] = back.reshape(heads, GROUP, KEYS)
        added = None
        for u in range(side):
            left = scores[:, rows[u], span].reshape(tall, n * KEYS)
            term = dot(left, jnp.concatenate(mixed[u], 1), NT)
            added = term if u == 0 else added + term
        sum_pre[...] += added
        return carry

    def rest(n):
        lax.fori_loop(0, ROWS // GROUP // SIDE_BACK[n], partial(group, n), 0)
        for p in range(pairs):
            at = p * LANES
            mine = slice(at, at + LANES)
            both = slice(2 * p, 2 * p + 2)
            queries = two_heads(qkv[pl.ds(row0, ROWS), mine], first_s, second_s).T
            grad = two_heads(grad_rows[:, mine], first_one, second_one).T
            back = grads[both, :, : n * KEYS].reshape(2 * ROWS, n * KEYS)
            out = dot(back, qkv[: n * KEYS, width + at : width + at + LANES])
            out = jnp.where(low, out[:ROWS], out[ROWS:]) * scaling
            grad_qkv[slot_of(step), mine, lanes] = out.T
            for kc in range(n):
                cols = slice(kc * KEYS, (kc + 1) * KEYS)
                to = slot_of(kc)
                grad_qkv[to, width + at : width + at + LANES, :] += dot(
                    queries, grads[both, :, cols].reshape(2 * ROWS, KEYS)
                )
                grad_qkv[to, 2 * width + at : 2 * width + at + LANES, :] += dot(
                    grad, weights[both, :, cols].reshape(2 * ROWS, KEYS)
                )

    for n in range(1, probs.shape[2] // KEYS + 1):
        pl.when(chunks == n)(partial(rest, n))

    @pl.when(step == pl.num_programs(0) - 1)
    def _():
        stay[...] = grad_qkv[:2]
        away[...] = grad_qkv[2:].astype(BF)
        row = lax.broadcasted_iota(jnp.int32, (tall, tall), 0)
        col = lax.broadcasted_iota(jnp.int32, (tall, tall), 1)
        same = row % GROUP == col % GROUP
        pick = (
            lax.broadcasted_iota(jnp.int32, (tall, LANES), 0) // GROUP
            == lax.broadcasted_iota(jnp.int32, (tall, LANES), 1)
        ).astype(F32)
        for source, out in ((sum_pre, grad_pre), (sum_post, grad_post)):
            kept = jnp.where(same, source[...], 0.0)
            wide = lax.dot_general(
                kept, pick, NN, precision=lax.Precision.HIGHEST, preferred_element_type=F32
            )
            for head in range(heads):
                out[head : head + 1, :] = jnp.sum(
                    wide[head * GROUP : (head + 1) * GROUP], axis=0, keepdims=True
                )


ANY = pl.BlockSpec(memory_space=pl.ANY)


def is_live(step, meta):
    return step * KEYS + meta[2] * ROWS < meta[0]


def attend(meta, sources, pre, post, heads, flops):
    width = sources[0].shape[1] // 3
    tall = heads * GROUP
    steps = 4
    full_len = steps * KEYS
    matrix = pl.BlockSpec((2 * tall, tall), lambda i, m: (0, 0), pipeline_mode=pl.Buffered(1))
    wide = pl.BlockSpec(
        (None, heads, ROWS, full_len), lambda i, m: (jnp.where(is_live(i, m), i, steps), 0, 0, 0)
    )
    kept = jax.ShapeDtypeStruct((steps + 1, heads, ROWS, full_len), BF)
    return pl.pallas_call(
        forward_kernel,
        grid_spec=pltpu.PrefetchScalarGridSpec(
            num_scalar_prefetch=1,
            grid=(steps,),
            in_specs=[ANY] * 4 + [matrix, matrix],
            out_specs=[
                pl.BlockSpec((None, ROWS, width), lambda i, m: (jnp.bitwise_xor(i, m[1]), 0, 0)),
                wide,
                wide,
            ],
            scratch_shapes=[
                pltpu.VMEM((full_len, 3 * width), BF),
                pltpu.VMEM((8, tall, full_len), F32),
                pltpu.SemaphoreType.DMA((4,)),
            ],
        ),
        out_shape=[jax.ShapeDtypeStruct((steps, ROWS, width), BF), kept, kept],
        compiler_params=pltpu.CompilerParams(vmem_limit_bytes=56 * 2**20),
        cost_estimate=pl.CostEstimate(
            flops=flops, bytes_accessed=1, transcendentals=0
        ),
        name="attend",
    )(meta, *sources, pre, post)


def attend_back(meta, sources, grad_rows, pre, post, probs, weights, flops):
    width = sources[0].shape[1] // 3
    steps = 4
    heads = probs.shape[1]
    tall = heads * GROUP
    full_len = steps * KEYS

    def newest(step, meta):
        last = 0
        for other in range(1, steps):
            last = jnp.where(is_live(other, meta), other, last)
        return jnp.minimum(step, last)

    matrix = pl.BlockSpec((2 * tall, tall), lambda i, m: (0, 0), pipeline_mode=pl.Buffered(1))
    wide = pl.BlockSpec((None, heads, ROWS, full_len), lambda i, m: (newest(i, m), 0, 0, 0))
    rows = pl.BlockSpec((None, ROWS, width), lambda i, m: (jnp.bitwise_xor(i, m[1]), 0, 0))
    small = pl.BlockSpec((heads, LANES), lambda i, m: (0, 0))
    pairs = pl.BlockSpec(
        (2, 3 * width, KEYS), lambda i, m: (0, 0, 0), pipeline_mode=pl.Buffered(1)
    )
    return pl.pallas_call(
        backward_kernel,
        grid_spec=pltpu.PrefetchScalarGridSpec(
            num_scalar_prefetch=1,
            grid=(steps,),
            in_specs=[ANY] * 4 + [rows, matrix, matrix, wide, wide],
            out_specs=[
                pairs,
                pairs,
                small,
                small,
            ],
            scratch_shapes=[
                pltpu.VMEM((full_len, 3 * width), BF),
                pltpu.VMEM((heads, ROWS, full_len), BF),
                pltpu.VMEM((heads, ROWS, full_len), BF),
                pltpu.VMEM((4, tall, full_len), F32),
                pltpu.VMEM((4, 3 * width, KEYS), F32),
                pltpu.VMEM((tall, tall), F32),
                pltpu.VMEM((tall, tall), F32),
                pltpu.SemaphoreType.DMA((4,)),
            ],
        ),
        out_shape=[
            jax.ShapeDtypeStruct((2, 3 * width, KEYS), F32),
            jax.ShapeDtypeStruct((2, 3 * width, KEYS), BF),
            jax.ShapeDtypeStruct((heads, LANES), F32),
            jax.ShapeDtypeStruct((heads, LANES), F32),
        ],
        compiler_params=pltpu.CompilerParams(vmem_limit_bytes=60 * 2**20),
        cost_estimate=pl.CostEstimate(
            flops=flops, bytes_accessed=1, transcendentals=0
        ),
        name="attend_back",
    )(meta, *sources, grad_rows, pre, post, probs, weights)


def gelu_both(value):
    scale = math.sqrt(2.0 / math.pi)
    square = value * value
    bent = jnp.tanh(scale * (value + 0.044715 * (square * value)))
    share = 0.5 * (1.0 + bent)
    slope = share + 0.5 * value * (1.0 - bent * bent) * (
        scale * (1.0 + 3.0 * 0.044715 * square)
    )
    return value * share, slope


def fill_weights(meta, sources, offs, inner, outer, proj, sems):
    hidden = inner.shape[1] // 2
    width = proj.shape[0]
    half = width // 2
    late, early = [], []

    def copy(source, target, kind=None):
        sem = sems.at[len(late) + len(early)]
        (late if kind is None else early).append(pltpu.make_async_copy(source, target, sem))

    count = len(sources) // 2
    for side in range(2):
        lanes = jnp.bitwise_xor(meta[1], side) * half
        to_proj = pl.ds(pl.multiple_of(lanes, LANES), half)
        to_inner = slice(side * hidden, (side + 1) * hidden)
        here = sources[count * side : count * side + count]
        if offs is None:
            copy(here[0], inner.at[:, to_inner])
            copy(here[1], proj.at[:, to_proj], 1)
            copy(here[2], outer.at[to_inner])
            continue
        own_rows = here[0].shape[1]
        folds = hidden * own_rows // width // own_rows
        for source, owners in zip(here, offs):
            for at_source, off in enumerate(owners):
                block = source.at[at_source]
                owner = jnp.bitwise_xor(meta[0], off)
                rows = pl.ds(pl.multiple_of(owner * own_rows, own_rows), own_rows)
                copy(block.at[:, :hidden], inner.at[rows, to_inner])
                copy(block.at[:, hidden : hidden + half], proj.at[rows, to_proj], 1)
                for fold in range(folds):
                    start = side * hidden + (owner * folds + fold) * own_rows
                    at = hidden + half + fold * width
                    copy(
                        block.at[:, at : at + width],
                        outer.at[pl.ds(pl.multiple_of(start, own_rows), own_rows)],
                    )
    for one in early + late:
        one.start()
    return early, late


TILE = 256
CHUNK = 512


def feed_kernel(offs, meta, gains, tokens, attended, grad_out, *refs):
    count = len(refs) - 17
    sources, refs = refs[:count], refs[count:]
    output, grad_resid, resid_low, grad_attended, gain_two, second_in = refs[:6]
    active, grad_hidden = refs[6:8], refs[8:10]
    inner, outer, proj, resid, out_sum, grad_sum, sems = refs[10:]
    rows = tokens.shape[0]
    step = pl.program_id(0)
    tiles = [slice(at, at + TILE) for at in range(0, rows, TILE)]

    @pl.when(step == 0)
    def _():
        early, late = fill_weights(meta, sources, offs, inner, outer, proj, sems)
        for one in early:
            one.wait()
        for tile in tiles:
            seq = meta[2 + tile.start // TILE]
            value = tokens[pl.ds(pl.multiple_of(seq * TILE, TILE), TILE)].astype(F32)
            value = value + dot(attended[tile], proj[...])
            resid[tile] = value
            out_sum[tile] = value
            grad_sum[tile] = jnp.zeros_like(value)
            second_in[tile] = (value * inverse_rms(value) * gains[1:2]).astype(BF)
        for one in late:
            one.wait()

    cols = pl.ds(pl.multiple_of(step * CHUNK, CHUNK), CHUNK)
    for tile in tiles:
        up = inner[:, cols]
        down = outer[cols]
        value, slope = gelu_both(dot(second_in[tile], up))
        value = value.astype(BF)
        back = (dot(grad_out[tile], down, NT) * slope).astype(BF)
        for side in range(2):

            @pl.when((step * 2 >= pl.num_programs(0)) == (side == 1))
            def _():
                active[side][tile] = value
                grad_hidden[side][tile] = back

        out_sum[tile] += dot(value, down)
        grad_sum[tile] += dot(back, up, NT)

    @pl.when(step == pl.num_programs(0) - 1)
    def _():
        gain_sum = jnp.zeros((8, proj.shape[0]), F32)
        for tile in tiles:
            seq = meta[2 + tile.start // TILE]
            output[pl.ds(pl.multiple_of(seq * TILE, TILE), TILE)] = out_sum[tile].astype(BF)
            value = resid[tile]
            scale = inverse_rms(value)
            normed = value * scale
            grad = grad_sum[tile]
            gain_sum += jnp.sum((grad * normed).reshape(TILE // 8, 8, -1), axis=0)
            back = grad_out[tile].astype(F32) + rms_backward(scale, normed, grad * gains[1:2])
            grad_resid[tile] = back
            back = back.astype(BF)
            resid_low[tile] = back
            grad_attended[tile] = dot(back, proj[...], NT).astype(BF)
        gain_two[...] = gain_sum


def feed_forward(meta, gains, tokens, attended, grad_out, sources, offs, hidden):
    rows, width = tokens.shape
    copies = 6
    if offs is not None:
        owners = sum(len(o) for o in offs)
        copies = 2 * owners * (2 + hidden // 2 // width)
    chunks = hidden // CHUNK

    def whole(shape):
        return pl.BlockSpec(shape, lambda c, m: (0,) * len(shape), pipeline_mode=pl.Buffered(1))

    flat = whole((rows, width))
    first = pl.BlockSpec((rows, CHUNK), lambda c, m: (0, jnp.minimum(c, chunks // 2 - 1)))
    second = pl.BlockSpec((rows, CHUNK), lambda c, m: (0, jnp.maximum(c - chunks // 2, 0)))
    wide = jax.ShapeDtypeStruct((rows, hidden // 2), BF)
    return pl.pallas_call(
        partial(feed_kernel, offs),
        grid_spec=pltpu.PrefetchScalarGridSpec(
            num_scalar_prefetch=1,
            grid=(chunks,),
            in_specs=[whole((2, width)), flat, flat, flat] + [ANY] * len(sources),
            out_specs=[flat, flat, flat, flat, whole((8, width)), flat, first, second, first, second],
            scratch_shapes=[
                pltpu.VMEM((width, hidden), BF),
                pltpu.VMEM((hidden, width), BF),
                pltpu.VMEM((width, width), BF),
                pltpu.VMEM((rows, width), F32),
                pltpu.VMEM((rows, width), F32),
                pltpu.VMEM((rows, width), F32),
                pltpu.SemaphoreType.DMA((copies,)),
            ],
        ),
        out_shape=[
            jax.ShapeDtypeStruct((rows, width), BF),
            jax.ShapeDtypeStruct((rows, width), F32),
            jax.ShapeDtypeStruct((rows, width), BF),
            jax.ShapeDtypeStruct((rows, width), BF),
            jax.ShapeDtypeStruct((8, width), F32),
            jax.ShapeDtypeStruct((rows, width), BF),
            wide,
            wide,
            wide,
            wide,
        ],
        compiler_params=pltpu.CompilerParams(vmem_limit_bytes=56 * 2**20),
        cost_estimate=pl.CostEstimate(
            flops=22 * 10**9, bytes_accessed=40 * 10**6, transcendentals=0
        ),
        name="feed_forward",
    )(meta, gains, tokens, attended, grad_out, *sources)


def weight_kernel(meta, second_in, attended, resid_low, grad_out, active, back, first, last, turned):
    width = second_in.shape[1]
    half = width // 2
    step = pl.program_id(0)

    @pl.when(step == 0)
    def _():
        turned[...] = second_in[...].T
        lanes = pl.ds(pl.multiple_of(meta[0] * half, LANES), half)
        hidden = first.shape[1] - half
        first[:, hidden:] = dot(attended[...], resid_low[:, lanes], TN).astype(first.dtype)

    cols = pl.ds(pl.multiple_of(step * CHUNK, CHUNK), CHUNK)
    first[:, cols] = dot(turned[...], back[...]).astype(first.dtype)
    last[...] = dot(active[...], grad_out[...], TN).astype(last.dtype)


def weight_sums(which, second_in, attended, resid_low, grad_out, active, back, kind):
    rows, width = second_in.shape
    hidden = active.shape[1]

    def whole(shape):
        return pl.BlockSpec(shape, lambda c, m: (0, 0), pipeline_mode=pl.Buffered(1))

    flat = whole((rows, width))
    chunk = pl.BlockSpec((rows, CHUNK), lambda c, m: (0, c))
    return pl.pallas_call(
        weight_kernel,
        grid_spec=pltpu.PrefetchScalarGridSpec(
            num_scalar_prefetch=1,
            grid=(hidden // CHUNK,),
            in_specs=[flat] * 4 + [chunk, chunk],
            out_specs=[
                whole((width, hidden + width // 2)),
                pl.BlockSpec((CHUNK, width), lambda c, m: (c, 0)),
            ],
            scratch_shapes=[pltpu.VMEM((width, rows), BF)],
        ),
        out_shape=[
            jax.ShapeDtypeStruct((width, hidden + width // 2), kind),
            jax.ShapeDtypeStruct((hidden, width), kind),
        ],
        compiler_params=pltpu.CompilerParams(vmem_limit_bytes=56 * 2**20),
        cost_estimate=pl.CostEstimate(flops=1, bytes_accessed=1, transcendentals=0),
        name="weight_sums",
    )(which, second_in, attended, resid_low, grad_out, active, back)


def squares_kernel(*refs):
    pairs, out = refs[:-1], refs[-1]
    total = jnp.zeros((8, LANES), F32)
    for at in range(0, len(pairs), 2):
        both = []
        for ref in pairs[at : at + 2]:
            rows, cols = ref.shape
            part = jnp.zeros((8, LANES), F32)
            value = ref[...]
            value = value * value
            value = jnp.sum(value.reshape(rows // 8, 8, cols), axis=0)
            for lane in range(0, cols, LANES):
                part = part + value[:, lane : lane + LANES]
            both.append(part)
        total = total + (both[0] + both[1])
    out[...] = total


def assemble_kernel(piece, meta, mine, other, last_mine, last_other, inner, proj, outer, out):
    squares_kernel(mine, other, last_mine, last_other, out)
    first = meta[0] == 0
    width = proj.shape[1]
    cut = inner.shape[1] // 2
    for which, (left, right) in enumerate(((mine, other), (other, mine))):

        @pl.when(first == (which == 0))
        def _():
            proj[:, : width // 2] = left[:, cut:]
            proj[:, width // 2 :] = right[:, cut:]
            for at in range(0, cut, piece):
                cols = slice(at, at + piece)
                inner[:, 2 * at : 2 * at + 2 * piece] = jnp.concatenate(
                    [left[:, cols], right[:, cols]], axis=1
                )

    for which, (left, right) in enumerate(((last_mine, last_other), (last_other, last_mine))):

        @pl.when(first == (which == 0))
        def _():
            rows = left.shape[0]
            outer[:rows] = left[...]
            outer[rows:] = right[...]


def assemble(core, piece, halves, last_halves):
    rows, wide = halves[0].shape
    last_rows, width = last_halves[0].shape
    vmem = pl.BlockSpec(memory_space=pltpu.VMEM)
    *found, squares = pl.pallas_call(
        partial(assemble_kernel, piece),
        in_specs=[pl.BlockSpec(memory_space=pltpu.SMEM)] + [vmem] * 4,
        out_specs=[vmem] * 4,
        out_shape=[
            jax.ShapeDtypeStruct((rows, 2 * wide - width), F32),
            jax.ShapeDtypeStruct((rows, width), F32),
            jax.ShapeDtypeStruct((2 * last_rows, width), F32),
            jax.ShapeDtypeStruct((8, LANES), F32),
        ],
        cost_estimate=pl.CostEstimate(flops=1, bytes_accessed=1, transcendentals=0),
        compiler_params=pltpu.CompilerParams(vmem_limit_bytes=40 * 2**20),
        name="assemble",
    )(core[None], *halves, *last_halves)
    return *found, jnp.sum(squares)


def squares_of(pairs):
    if any(v.shape[0] % 8 for pair in pairs for v in pair):
        found = [jnp.sum(a * a) + jnp.sum(b * b) for a, b in pairs]
        return sum(found[1:], found[0])
    vmem = pl.BlockSpec(memory_space=pltpu.VMEM)
    flat = [v for pair in pairs for v in pair]
    out = pl.pallas_call(
        squares_kernel,
        in_specs=[vmem] * len(flat),
        out_specs=vmem,
        out_shape=jax.ShapeDtypeStruct((8, LANES), F32),
        cost_estimate=pl.CostEstimate(flops=1, bytes_accessed=1, transcendentals=0),
        compiler_params=pltpu.CompilerParams(vmem_limit_bytes=40 * 2**20),
        name="squares",
    )(*flat)
    return jnp.sum(out)


RATES = (0.03, 0.1, 0.03, 0.02, 0.3)


def adamw_kernel(factor, *refs):
    count = len(RATES)
    grads, states, outs = refs[:count], refs[count : 5 * count], refs[5 * count :]

    def update(at):
        scaled = grads[at][...] * factor[0]
        new = adamw(*[r[...] for r in states[4 * at : 4 * at + 4]], scaled, RATES[at])
        for out, value in zip(outs[4 * at : 4 * at + 4], new):
            out[...] = value

    for at in range(4):
        update(at)

    @pl.when(pl.program_id(0) == 0)
    def _():
        for at in range(4, count):
            update(at)


def adamw_all(factor, grads, states):
    steps = 6

    def block(at, shape):
        if at >= 4:
            return pl.BlockSpec(shape, lambda i: (0,) * len(shape))
        if at == 3:
            return pl.BlockSpec((shape[0] // steps, shape[1]), lambda i: (i, 0))
        return pl.BlockSpec((shape[0], shape[1] // steps), lambda i: (0, i))

    specs = [block(at, g.shape) for at, g in enumerate(grads)]
    wide = [s for s in specs for _ in range(4)]
    out = pl.pallas_call(
        adamw_kernel,
        grid=(steps,),
        in_specs=[pl.BlockSpec(memory_space=pltpu.SMEM)] + specs + wide,
        out_specs=wide,
        out_shape=[jax.ShapeDtypeStruct(g.shape, F32) for g in grads for _ in range(4)],
        compiler_params=pltpu.CompilerParams(vmem_limit_bytes=62 * 2**20),
        name="adamw_all",
    )(factor, *grads, *[v for state in states for v in state])
    return out


def first_kernel(offs, wanted, blocks, meta, tokens, *refs):
    count = 2 * (1 if offs is None else len(offs))
    sources, refs = refs[:count], refs[count:]
    outs, (first_in, gains, weight, mixed, sems) = refs[: len(wanted)], refs[len(wanted) :]
    side = weight.shape[1] // 2
    copies = []

    def copy(source, target):
        copies.append(pltpu.make_async_copy(source, target, sems.at[len(copies)]))

    for which in range(2):
        here = sources[which * (count // 2) : (which + 1) * (count // 2)]
        start = pl.multiple_of(jnp.bitwise_xor(meta[1], which) * side, side)
        if offs is None:
            copy(here[0].at[:, :side], weight.at[:, pl.ds(start, side)])
            if which == 0:
                copy(here[0].at[:, side:], mixed)
            continue
        own_rows = here[0].shape[1]
        for source, owners in zip(here, offs):
            for at, off in enumerate(owners):
                owner = jnp.bitwise_xor(meta[0], off)
                rows = pl.ds(pl.multiple_of(owner * own_rows, own_rows), own_rows)
                copy(source.at[at, :, :side], weight.at[rows, pl.ds(start, side)])
                if which == 0:
                    copy(source.at[at, :, side:], mixed.at[rows])
    for one in copies:
        one.start()
    for one in copies:
        one.wait()
    gain = mixed[...].astype(F32).T[:8]
    gains[...] = gain
    for block in range(blocks):
        value = tokens[meta[2 + block]].astype(F32)
        low = (value * inverse_rms(value) * gain[:1]).astype(BF)
        first_in[block * KEYS : (block + 1) * KEYS] = low
        if block not in wanted:
            continue
        out = outs[wanted.index(block)]
        wide = 2 * side // 3
        for col in range(0, 2 * side, wide):
            cols = slice(col, col + wide)
            out[:, cols] = dot(low, weight[:, cols]).astype(BF)


def first_product(meta, tokens, pieces, offs, wanted, blocks, with_weight):
    width = tokens.shape[2]
    rows = blocks * KEYS
    vmem = pl.BlockSpec(memory_space=pltpu.VMEM)
    out_shape = [
        *[jax.ShapeDtypeStruct((KEYS, 3 * width), BF) for _ in wanted],
        jax.ShapeDtypeStruct((rows, width), BF),
        jax.ShapeDtypeStruct((8, width), F32),
    ]
    scratch = [
        pltpu.VMEM((width, LANES), BF),
        pltpu.SemaphoreType.DMA((3 if offs is None else 3 * sum(len(o) for o in offs),)),
    ]
    if with_weight:
        out_shape.append(jax.ShapeDtypeStruct((width, 3 * width), BF))
    else:
        scratch = [pltpu.VMEM((width, 3 * width), BF)] + scratch
    return pl.pallas_call(
        partial(first_kernel, offs, wanted, blocks),
        in_specs=[pl.BlockSpec(memory_space=pltpu.SMEM), vmem] + [ANY] * len(pieces),
        out_specs=[vmem] * len(out_shape),
        out_shape=out_shape,
        scratch_shapes=scratch,
        compiler_params=pltpu.CompilerParams(vmem_limit_bytes=40 * 2**20),
        cost_estimate=pl.CostEstimate(
            flops=1, bytes_accessed=1, transcendentals=0
        ),
        name="first_product",
    )(meta, tokens, *pieces)


def first_grads_kernel(meta, first_in, *refs):
    cols, (out,) = refs[:-1], refs[-1:]
    side = out.shape[1]
    take = pl.ds(pl.multiple_of(meta[0] * side, side), side)
    total = None
    for block, grads in enumerate(cols):
        rows = first_in[block * KEYS : (block + 1) * KEYS].T
        term = dot(rows, grads[take], NT)
        total = term if block == 0 else total + term
        if block + 1 < len(cols):
            continue
        out[...] = total.astype(out.dtype)


def first_grads(which, first_in, cols, kind):
    width = first_in.shape[1]
    side = cols[0].shape[0] // 2
    vmem = pl.BlockSpec(memory_space=pltpu.VMEM)
    return pl.pallas_call(
        first_grads_kernel,
        in_specs=[pl.BlockSpec(memory_space=pltpu.SMEM)] + [vmem] * (1 + len(cols)),
        out_specs=vmem,
        out_shape=jax.ShapeDtypeStruct((width, side), kind),
        compiler_params=pltpu.CompilerParams(vmem_limit_bytes=50 * 2**20),
        cost_estimate=pl.CostEstimate(
            flops=1, bytes_accessed=1, transcendentals=0
        ),
        name="first_grads",
    )(which, first_in, *cols)


def token_grads_kernel(meta, gains, near, far, weight, tokens, grad_resid, *refs):
    out, gain_out = refs[-2:]
    step = pl.program_id(0)

    @pl.when(step == 0)
    def _():
        gain_out[...] = jnp.zeros_like(gain_out)

    for which, grads in enumerate((near, far)):

        @pl.when(step == which)
        def _():
            back = dot(weight[...], grads[...]).T
            value = tokens[...].astype(F32)
            scale = inverse_rms(value)
            normed = value * scale
            gain_out[...] += jnp.sum((back * normed).reshape(KEYS // 8, 8, -1), axis=0)
            out[...] = grad_resid[...] + rms_backward(scale, normed, back * gains[:1])


def token_grads(slot, seqs, gains, near, far, weight, tokens, grad_resid, before):
    _, rows, width = tokens.shape

    def whole(shape):
        return pl.BlockSpec(shape, lambda i, m: (0,) * len(shape), pipeline_mode=pl.Buffered(1))

    place = pl.BlockSpec((None, rows, width), lambda i, m: (m[i], 0, 0))
    extra = [] if before is None else [before]
    return pl.pallas_call(
        token_grads_kernel,
        grid_spec=pltpu.PrefetchScalarGridSpec(
            num_scalar_prefetch=1,
            grid=(2,),
            in_specs=[
                whole(gains.shape),
                whole(near.shape),
                whole(far.shape),
                whole(weight.shape),
                place,
                pl.BlockSpec((None, rows, width), lambda i, m: (2 * slot + i, 0, 0)),
            ]
            + [ANY] * len(extra),
            out_specs=[place, whole((8, width))],
        ),
        out_shape=[
            jax.ShapeDtypeStruct(tokens.shape, F32),
            jax.ShapeDtypeStruct((8, width), F32),
        ],
        input_output_aliases={7: 0} if extra else {},
        compiler_params=pltpu.CompilerParams(vmem_limit_bytes=50 * 2**20),
        cost_estimate=pl.CostEstimate(
            flops=1, bytes_accessed=1, transcendentals=0
        ),
        name="token_grads",
    )(seqs, gains, near, far, weight, tokens, grad_resid, *extra)


def prepare_kernel(owners, meta, inner, outer, proj, out):
    rows, hidden = inner.shape
    width = proj.shape[1]
    half = width // 2
    piece = hidden // owners // 2
    for core in range(2):

        @pl.when(meta[1] == core)
        def _():
            for owner in range(owners):
                at = (2 * owner + core) * piece
                out[:, owner * piece : (owner + 1) * piece] = inner[:, at : at + piece].astype(BF)
            cut = hidden // 2
            out[:, cut : cut + half] = proj[:, core * half : (core + 1) * half].astype(BF)
            for fold in range(piece // rows):
                at = core * piece + fold * rows
                start = cut + half + fold * width
                out[:, start : start + width] = outer[at : at + rows].astype(BF)


def prepare(meta, owners, inner, outer, proj):
    rows, hidden = inner.shape
    width = proj.shape[1]
    vmem = pl.BlockSpec(memory_space=pltpu.VMEM)
    return pl.pallas_call(
        partial(prepare_kernel, owners),
        in_specs=[pl.BlockSpec(memory_space=pltpu.SMEM)] + [vmem] * 3,
        out_specs=vmem,
        out_shape=jax.ShapeDtypeStruct((rows, hidden + width // 2), BF),
        cost_estimate=pl.CostEstimate(flops=1, bytes_accessed=1, transcendentals=0),
        compiler_params=pltpu.CompilerParams(vmem_limit_bytes=40 * 2**20),
        name="prepare",
    )(meta, inner, outer, proj)


def on_device(
    tokens,
    cotangent,
    lengths,
    qkv_weight,
    qkv_first,
    qkv_second,
    qkv_average,
    proj_weight,
    proj_first,
    proj_second,
    proj_average,
    inner_weight,
    inner_first,
    inner_second,
    inner_average,
    outer_weight,
    outer_first,
    outer_second,
    outer_average,
    gains,
    gain_first,
    gain_second,
    gain_average,
    mixes,
    mix_first,
    mix_second,
    mix_average,
):
    group_seqs, shard_len, width = tokens.shape
    owners = lax.axis_size("dp")
    heads = mixes.shape[1]
    own_rows = qkv_weight.shape[0]
    hidden = inner_weight.shape[1]
    half = width // 2
    slice_ff = hidden // owners // 2
    me = lax.axis_index("seq")
    pair = me // 2
    core = jnp.bitwise_and(me, 1)

    def by_core(mine, other, axis):
        return jnp.where(
            core == 0,
            jnp.concatenate([mine, other], axis),
            jnp.concatenate([other, mine], axis),
        )

    ahead = (lengths[None, :] > lengths[:, None]) | (
        (lengths[None, :] == lengths[:, None])
        & (jnp.arange(group_seqs)[None, :] < jnp.arange(group_seqs)[:, None])
    )
    rank = jnp.sum(ahead.astype(jnp.int32), axis=1)
    def by_rank(place, values):
        return jnp.sum(jnp.where(rank == place, values, 0)).astype(jnp.int32)

    def of_slot(slot, which, values):
        first, second = (0, 1) if slot == 0 else (group_seqs - 1, group_seqs - 2)
        return jnp.where(which == 0, by_rank(first, values), by_rank(second, values))

    def sequence_of(slot, which):
        return of_slot(slot, which, jnp.arange(group_seqs, dtype=jnp.int32))

    def pack(values):
        spot = jnp.arange(len(values), dtype=jnp.int32)
        total = jnp.zeros((len(values),), jnp.int32)
        for at, value in enumerate(values):
            total = jnp.where(spot == at, value, total)
        return total

    def arrange(value):
        return jnp.stack(
            [
                jnp.stack(
                    [
                        lax.dynamic_index_in_dim(
                            value, sequence_of(slot, jnp.bitwise_xor(pair, d)), 0, False
                        )
                        for d in range(2)
                    ]
                )
                for slot in range(2)
            ]
        )

    lengths_here = [[of_slot(s, jnp.bitwise_xor(pair, d), lengths) for d in range(2)] for s in range(2)]
    seqs = [pack([sequence_of(s, pair), sequence_of(s, 1 - pair)]) for s in range(2)]
    feed_meta = pack(
        [lax.axis_index("dp"), core]
        + [sequence_of(s, jnp.bitwise_xor(pair, d)) for s in range(2) for d in range(2)]
    )
    metas = [pack([lengths_here[slot][0], me, core]) for slot in range(2)]

    mixers = spread(mixes)
    positions = me * shard_len + jnp.arange(shard_len, dtype=jnp.int32)
    used = jnp.stack([jnp.stack(found) for found in lengths_here])
    live = positions[None, None, :] < used[:, :, None]
    cot = arrange(cotangent)
    grad_out = jnp.where(live[..., None], cot, jnp.zeros_like(cot))
    folds = slice_ff // own_rows
    if own_rows % 16 == 0:
        rest = prepare(feed_meta, owners, inner_weight, outer_weight, proj_weight)[None]
    else:
        inner_mine = inner_weight.astype(BF).reshape(own_rows, owners, 2, slice_ff)
        inner_mine = lax.dynamic_index_in_dim(inner_mine, core, 2, False)
        outer_mine = outer_weight.astype(BF).reshape(2, folds, own_rows, width)
        outer_mine = lax.dynamic_index_in_dim(outer_mine, core, 0, False)
        rest = jnp.concatenate(
            [
                inner_mine.reshape(own_rows, owners * slice_ff),
                lax.dynamic_slice_in_dim(proj_weight.astype(BF), core * half, half, 1),
            ]
            + [outer_mine[f] for f in range(folds)],
            axis=1,
        )[None]
    side = qkv_weight.shape[1] // 2
    mine = lax.dynamic_slice_in_dim(qkv_weight.astype(BF), core * side, side, 1)
    mine = jnp.concatenate([mine, jnp.pad(gains.astype(BF).T, ((0, 0), (0, LANES - 2)))], 1)
    offs = None
    if owners == 8:
        shard = mine[None]
        got = swap(shard, "dp", 4)
        got = after(got, feed_meta, rest)
        pieces = [jnp.concatenate([shard, got])]
        far_z, far_x = swap(pieces[0], "dp", 2), swap(pieces[0], "dp", 1)
        beside = [swap(pieces[0], "seq", 1)]
        pieces += [far_z, far_x]
        pieces.append(swap(far_z, "dp", 1))
        beside += [swap(p, "seq", 1) for p in pieces[1:]]
        offs = ((0, 4), (2, 6), (1, 5), (3, 7))
        pieces += beside
        late = far_z
    else:
        mine = lax.all_gather(mine, "dp", axis=0, tiled=True)
        pieces = [mine, swap(mine, "seq", 1)]

    if offs is not None:
        got = swap(after(rest, late), "dp", 4)
    place = feed_meta
    near, far, *_ = first_product(
        place, tokens, pieces, offs, (0, 1), 2, False
    )
    near, far = [near], [far]
    here = swap(far[0], "seq", 2)
    beside = swap(near[0], "seq", 1)
    place, beside, mixers, metas, grad_out = lax.optimization_barrier(
        (place, beside, mixers, metas, grad_out)
    )
    pre_mix, post_mix, pre_back, post_back = mixers
    *out, first_in, gain_vals, weight_qkv = first_product(
        place, tokens, pieces, offs, (2, 3), 4, True
    )
    near.append(out[0])
    far.append(out[1])
    here = after(here, far[1], near[1])
    if offs is not None:
        here, got = lax.optimization_barrier((here, got))
        rest_pieces = [jnp.concatenate([rest, got])]
        far_z, far_x = swap(rest_pieces[0], "dp", 2), swap(rest_pieces[0], "dp", 1)
    sources = [[near[0], beside, here, swap(here, "seq", 1)]]
    next_far = swap(after(far[1], here), "seq", 2)
    beside = swap(after(near[1], here), "seq", 1)
    def by_half(rows):
        return jnp.where(core == 0, rows, rows[:, ::-1])

    rows, probs, weights = [None, None], [None, None], [None, None]
    meta = after(metas[0], sources[0])
    if offs is not None:
        meta = after(meta, rest_pieces)
        beside_rest = [swap(rest_pieces[0], "seq", 1)]
    rows[0], probs[0], weights[0] = attend(meta, sources[0], pre_mix, post_mix, heads, FLOPS[0])
    next_far, beside = lax.optimization_barrier((next_far, beside, rows[0]))[:2]
    if offs is not None:
        far_z, far_x, next_far, beside, beside_rest = lax.optimization_barrier(
            (far_z, far_x, next_far, beside, beside_rest)
        )
        rest_pieces += [far_z, far_x]
        beside_rest = list(beside_rest) + [swap(p, "seq", 1) for p in (far_z, far_x)]
        last = swap(far_z, "dp", 1)
    sources.append([near[1], beside, next_far, swap(next_far, "seq", 1)])
    far_rows = swap(rows[0][2:], "seq", 2)
    rows[1], probs[1], weights[1] = attend(
        metas[1], sources[1], pre_mix, post_mix, heads, FLOPS[1]
    )
    far_rows = after(far_rows, rows[1])
    cut = owners * slice_ff + half
    if offs is not None:
        last, *beside_rest = after([last] + beside_rest, rows[1])
        rest_pieces.append(last)
        feed_weights = rest_pieces + beside_rest + [swap(last, "seq", 1)]
    else:
        rest = lax.all_gather(rest[0], "dp")
        feed_weights = []
        for part in (rest, swap(rest, "seq", 1)):
            flat = part.reshape(owners * own_rows, -1)
            down = jnp.moveaxis(part[:, :, cut:].reshape(owners, own_rows, folds, width), 2, 1)
            feed_weights += [
                flat[:, : cut - half],
                flat[:, cut - half : cut],
                down.reshape(owners * slice_ff, width),
            ]
    far_rows = jnp.stack([far_rows, swap(rows[1][2:], "seq", 2)])
    near_rows = jnp.stack([rows[0][1], rows[1][1]])
    got = swap(jnp.stack([near_rows, far_rows[:, 1]]), "seq", 1)
    attention_output = jnp.stack(
        [
            by_half(
                jnp.stack(
                    [
                        jnp.stack([rows[slot][0], got[0, slot]]),
                        jnp.stack([far_rows[slot, 0], got[1, slot]]),
                    ]
                )
            ).reshape(2, 2 * ROWS, width)
            for slot in range(2)
        ]
    )

    flat = (-1, width)
    attention_output = attention_output.reshape(flat)
    flat_out = grad_out.reshape(flat)
    output, grad_resid, resid_low, grad_attended, gain_two, second_in, *wide = feed_forward(
        feed_meta,
        gain_vals[:2],
        tokens.reshape(flat),
        attention_output,
        flat_out,
        feed_weights,
        offs,
        hidden,
    )
    grad_attended = grad_attended.reshape(grad_out.shape)
    grad_resid = grad_resid.reshape(4, shard_len, width)

    def sums_of(side, which, kind):
        return weight_sums(
            which[None],
            second_in,
            attention_output,
            resid_low,
            flat_out,
            wide[side],
            wide[2 + side],
            kind,
        )

    output = output.reshape(tokens.shape)
    gain_two = jnp.sum(gain_two, axis=0)

    sent = sums_of(1, 1 - core, BF)
    arrived = swap(sent[0], "seq", 1), swap(sent[1], "seq", 1)
    meta = after(core, sent)
    mine = sums_of(0, meta, F32)
    arrived = after(arrived, mine, output)
    twos = [(2**k, 2) for k in range(owners.bit_length() - 1)]
    orders = [twos, twos[1:2] + twos[:1] + twos[2:]]
    chains = []
    for at in range(2):
        total = (mine[at] + arrived[at].astype(F32)).astype(BF)
        total = total.reshape((2,) * len(twos) + (-1, total.shape[1]))
        chains.append(split_blocks(total, "dp", twos[::-1], orders[at][0]))

    def send_step(at, turn, parts):
        stride, radix = orders[at][turn]
        return tuple(swap(parts[0][k], "dp", k * stride) for k in range(1, radix))

    def join_step(at, turn, parts, got):
        total = parts[0][0].astype(F32)
        for part in got:
            total = total + part.astype(F32)
        if turn + 1 == len(twos):
            return total
        return split_blocks(total.astype(BF), "dp", parts[1], orders[at][turn + 1])

    def step_on(at, turn, parts, *first):
        got = send_step(at, turn, parts)
        return join_step(at, turn, parts, after(got, *first) if first else got)

    def to_far(slot):
        found = by_half(grad_attended[slot].reshape(2, 2, ROWS, width)).reshape(4, ROWS, width)
        return found, swap(found[2:], "seq", 2)

    def from_near(found, far):
        got = swap(jnp.stack([found[1], far[1]]), "seq", 1)
        return jnp.stack([found[0], got[0], far[0], got[1]])

    def attend_slot(slot, meta, rows):
        return attend_back(
            meta, sources[slot], rows, pre_back, post_back, probs[slot], weights[slot], FLOPS[slot]
        )

    found, far = to_far(0)
    far = after(far, mine)
    next_found, next_far = to_far(1)
    meta = after(metas[0], chains)
    stay, away, back_pre, back_post = attend_slot(0, meta, from_near(found, far))
    grad_mixes = jnp.stack([back_pre[:, :heads], back_post[:, :heads]])
    chains = [step_on(at, 0, chains[at], stay) for at in range(2)]
    away, next_far = lax.optimization_barrier((away, next_far, chains))[:2]
    next_rows = from_near(next_found, next_far)
    summed = (stay + swap(away, "seq", 1).astype(F32)).astype(BF)
    far = swap(summed[1], "seq", 2)
    meta = after(metas[1], summed, chains)
    stay, away, back_pre, back_post = attend_slot(1, meta, next_rows)
    grad_mixes = grad_mixes + jnp.stack([back_pre[:, :heads], back_post[:, :heads]])
    got = [send_step(at, 1, chains[at]) for at in range(2)]
    away, far, got = lax.optimization_barrier((away, far, got, stay))[:3]
    grad_cols = [(summed[0], far)]
    summed = (stay + swap(away, "seq", 1).astype(F32)).astype(BF)
    got = after(got, summed)
    chains = [join_step(at, 1, chains[at], got[at]) for at in range(2)]
    far = swap(summed[1], "seq", 2)

    def to_tokens(slot, before, first):
        return token_grads(
            slot,
            after(seqs[slot], first),
            gain_vals,
            *grad_cols[slot],
            weight_qkv,
            tokens,
            grad_resid,
            before,
        )

    begun = to_tokens(0, None, summed)
    for turn in range(2, len(twos)):
        chains = [step_on(at, turn, chains[at], begun) for at in range(2)]
    first_part, second_part = chains
    others = first_part.astype(BF), second_part.astype(BF)
    far, begun, others = lax.optimization_barrier((far, begun, others))
    grad_cols.append((summed[0], far))
    cols = grad_cols[0] + grad_cols[1]
    sent = first_grads((1 - core)[None], first_in, cols, BF)
    qkv_mine = first_grads(after(core, sent)[None], first_in, cols, F32)

    def over_pairs(total, *first):
        total = lax.optimization_barrier(jax.tree.map(lambda v: v.astype(BF), total))
        got = jax.tree.map(lambda v: swap(v, "seq", 2), total)
        if first:
            got = after(got, *first)
        return jax.tree.map(lambda v, w: v.astype(F32) + w.astype(F32), total, got)

    arrived = after(swap(sent, "seq", 1), qkv_mine)
    qkv_total = (qkv_mine + arrived.astype(F32)).astype(BF)
    qkv_total = qkv_total.reshape((2,) * len(twos) + (own_rows, side))
    third = side // LANES // 3 * LANES
    chains = [qkv_total[..., third:], qkv_total[..., :third]]
    chains = [split_blocks(chains[at], "dp", twos[::-1], orders[at][0]) for at in range(2)]
    others = over_pairs(after(others, [p for p, _ in chains]))
    got = [send_step(at, 0, chains[at]) for at in range(2)]
    grad_rows_tokens, gain_more = to_tokens(1, begun[0], got[1])
    got[0] = after(got[0], grad_rows_tokens)
    chains = [join_step(at, 0, chains[at], got[at]) for at in range(2)]
    got = [send_step(at, 1, chains[at]) for at in range(2)]
    gain_one = jnp.sum(begun[1] + gain_more, axis=0)
    small = jnp.concatenate([gain_one, gain_two, grad_mixes.reshape(-1)])
    count = small.shape[0]
    small = jnp.pad(small, (0, -(count + 1) % (8 * LANES) + 1)).reshape(-1, LANES)
    chains = [join_step(at, 1, chains[at], got[at]) for at in range(2)]

    first_halves = (others[0], swap(others[0], "seq", 1))
    last_halves = (others[1], swap(others[1], "seq", 1))
    if own_rows % 8 == 0:
        red_inner, red_proj, red_outer, squares = assemble(
            core, slice_ff, first_halves, last_halves
        )
    else:
        red_proj = by_core(*[g[:, cut - half :] for g in first_halves], 1)
        red_inner = by_core(
            *[g[:, : cut - half].reshape(own_rows, owners, 1, slice_ff) for g in first_halves], 2
        ).reshape(own_rows, hidden)
        red_outer = by_core(*last_halves, 0)
        squares = squares_of([first_halves, last_halves])
    small = small + swap(small, "seq", 1)
    small = small + swap(small, "seq", 2)
    pins = (red_inner, red_proj, red_outer, squares)
    for turn in range(2, len(twos)):
        chains = [step_on(at, turn, chains[at], *pins) for at in range(2)]
        pins = ()
    qkv_total = over_pairs(jnp.concatenate(chains[::-1], axis=-1), small)
    qkv_other = swap(qkv_total, "seq", 1)
    red_qkv = by_core(qkv_total, qkv_other, 1)

    squares = squares + squares_of([(qkv_total, qkv_other)])
    place = lax.broadcasted_iota(jnp.int32, small.shape, 0) * LANES
    place = place + lax.broadcasted_iota(jnp.int32, small.shape, 1)
    small = sum_everywhere(jnp.where(place == count, squares, small), "dp").reshape(-1)
    gain_all = small[: 2 * width].reshape(2, width)
    red_gains = lax.dynamic_slice_in_dim(gain_all, lax.axis_index("dp") * own_rows, own_rows, 1)
    red_mixes = small[2 * width : count].reshape(mixes.shape)
    grad_norm = jnp.sqrt(
        small[count] + jnp.sum(gain_all * gain_all) + jnp.sum(red_mixes * red_mixes)
    )
    factor = CLIP / jnp.maximum(grad_norm, CLIP)
    clipped_gains = red_gains * factor
    new = adamw_all(
        factor[None],
        (red_qkv, red_proj, red_inner, red_outer, red_gains),
        (
            (qkv_weight, qkv_first, qkv_second, qkv_average),
            (proj_weight, proj_first, proj_second, proj_average),
            (inner_weight, inner_first, inner_second, inner_average),
            (outer_weight, outer_first, outer_second, outer_average),
            (gains, gain_first, gain_second, gain_average),
        ),
    )
    mix_new = adamw(mixes, mix_first, mix_second, mix_average, red_mixes * factor, 0.3)
    return (
        output,
        grad_rows_tokens,
        grad_norm,
        *new,
        *mix_new,
        clipped_gains,
    )


def solution(mesh):
    rows = P("dp", "seq", None)
    matrix = P("dp", None)
    vector = P(None, "dp")
    in_specs = (rows, rows, P("dp")) + (matrix,) * 16 + (vector,) * 4 + (P(),) * 4
    out_specs = (rows, rows, P()) + (matrix,) * 16 + (vector,) * 4 + (P(),) * 4 + (vector,)
    return jax.shard_map(
        on_device, mesh=mesh, in_specs=in_specs, out_specs=out_specs, check_vma=False
    )
```

profile of v0, /device:TPU:0, one launch (start us, length us, event | category | flops | bytes accessed | tf_op | source)
XLA Modules:
  0.0 497.7 jit_solution(1449820985594619707)
XLA Ops:
  21.5 9.6 %collective-permute-done.1.refs_1_ = bf16[2,96,1280]{2,1,0:T(8,128)(2,1)S(1)} collective-permute-done((bf16[2,96,1280]{2,1,0:T(8,128)(2,1)S(1)}, bf16[2,96,1280]{2,1,0:T(8,128)(2,1)S(1)}, u32[]{:S(2)}, u32[]{:S(2)}) %collective-permute-start.1) | collective-permute-done | bytes 491552 | tf_op jit(solution)/shard_map/ppermute | solution.py:61
  33.1 10.0 %collective-permute-done.3.refs_3_ = bf16[2,96,1280]{2,1,0:T(8,128)(2,1)} collective-permute-done((bf16[2,96,1280]{2,1,0:T(8,128)(2,1)S(1)}, bf16[2,96,1280]{2,1,0:T(8,128)(2,1)}, u32[]{:S(2)}, u32[]{:S(2)}) %collective-permute-start.3) | collective-permute-done | bytes 491552 | tf_op jit(solution)/shard_map/ppermute | solution.py:61
  45.3 6.2 %first_product.2 = (bf16[256,2304]{1,0:T(8,128)(2,1)}, bf16[256,2304]{1,0:T(8,128)(2,1)}, bf16[512,768]{1,0:T(8,128)(2,1)}, f32[8,768]{1,0:T(8,128)}) custom-call(s32[6]{0:T(128)S(1)} %compare_select_fusion.5.meta, bf16[4,256,768]{2,1,0:T(8,128)(2,1)S(1)} %copy-done, bf16[2,96,1280]{2,1,0:T(8,128)(2,1)S(1)} %pad_maximum_fusion.7.refs_0_, ...), custom_call_target="tpu_custom_call" | custom-call | flops 1 | bytes 1 | tf_op jit(solution)/shard_map/first_product/pallas_call | solution.py:920
  71.2 5.3 %first_product.3 = (bf16[256,2304]{1,0:T(8,128)(2,1)S(1)}, bf16[256,2304]{1,0:T(8,128)(2,1)S(1)}, bf16[1024,768]{1,0:T(8,128)(2,1)S(1)}, f32[8,768]{1,0:T(8,128)S(1)}, bf16[768,2304]{1,0:T(8,128)(2,1)S(1)}) custom-call(s32[6]{0:T(128)S(1)} %compare_select_fusion.5.meta, bf16[4,256,768]{2,1,0:T(8,128)(2,1)S(1)} %copy-done, ...), custom_call_target="tpu_custom_call" | custom-call | flops 1 | bytes 1 | tf_op jit(solution)/shard_map/first_product/pallas_call | solution.py:920
  80.2 14.0 %collective-permute-done.10 = bf16[1,96,3456]{2,1,0:T(8,128)(2,1)} collective-permute-done((bf16[1,96,3456]{2,1,0:T(8,128)(2,1)S(1)}, bf16[1,96,3456]{2,1,0:T(8,128)(2,1)}, u32[]{:S(2)}, u32[]{:S(2)}) %collective-permute-start.10) | collective-permute-done | bytes 663584 | tf_op jit(solution)/shard_map/ppermute | solution.py:61
  98.7 24.9 %attend.2 = (bf16[4,128,768]{2,1,0:T(8,128)(2,1)}, bf16[5,12,128,1024]{3,2,1,0:T(8,128)(2,1)}, bf16[5,12,128,1024]{3,2,1,0:T(8,128)(2,1)}) custom-call(s32[3]{0:T(128)} %get-tuple-element.214.meta, bf16[256,2304]{1,0:T(8,128)(2,1)} %get-tuple-element.161.refs_0_, bf16[256,2304]{1,0:T(8,128)(2,1)} %collective-permute-done.8.refs_1_, ...), custom_call_target="tpu_custom_call" | custom-call | flops 60000002048 | bytes 1 | tf_op jit(solution)/shard_map/attend/pallas_call | solution.py:427
  132.5 16.1 %attend.3 = (bf16[4,128,768]{2,1,0:T(8,128)(2,1)}, bf16[5,12,128,1024]{3,2,1,0:T(8,128)(2,1)}, bf16[5,12,128,1024]{3,2,1,0:T(8,128)(2,1)}) custom-call(s32[3]{0:T(128)} %get-tuple-element.226.meta, bf16[256,2304]{1,0:T(8,128)(2,1)} %copy-done.13, bf16[256,2304]{1,0:T(8,128)(2,1)} %copy-done.20, bf16[256,2304]{1,0:T(8,128)(2,1)} %copy-done.21, ...), custom_call_target="tpu_custom_call" | custom-call | flops 1 | bytes 1 | tf_op jit(solution)/shard_map/attend/pallas_call | solution.py:427
  151.4 9.1 %collective-permute-done.19 = bf16[2,128,768]{2,1,0:T(8,128)(2,1)S(1)} collective-permute-done((bf16[2,128,768]{2,1,0:T(8,128)(2,1)S(1)}, bf16[2,128,768]{2,1,0:T(8,128)(2,1)S(1)}, u32[]{:S(2)}, u32[]{:S(2)}) %collective-permute-start.19) | collective-permute-done | bytes 393248 | tf_op jit(solution)/shard_map/ppermute | solution.py:61
  166.2 43.9 %feed_forward.1 = (bf16[1024,768]{1,0:T(8,128)(2,1)}, f32[1024,768]{1,0:T(8,128)}, bf16[1024,768]{1,0:T(8,128)(2,1)}, bf16[1024,768]{1,0:T(8,128)(2,1)}, f32[8,7...) custom-call(s32[6]{0:T(128)} %copy-done.18, ...), custom_call_target="tpu_custom_call" | custom-call | flops 22000001024 | bytes 40000000 | tf_op jit(solution)/shard_map/feed_forward/pallas_call | solution.py:644
  210.2 11.5 %weight_sums.2 = (bf16[768,1920]{1,0:T(8,128)(2,1)}, bf16[1536,768]{1,0:T(8,128)(2,1)}) custom-call(s32[1]{0:T(128)} %bitcast.31.meta, bf16[1024,768]{1,0:T(8,128)(2,1)} %get-tuple-element.201.second_in, bf16[1024,768]{1,0:T(8,128)(2,1)} %bitcast.159, bf16[1024,768]{1,0:T(8,128)(2,1)} %get-tuple-element.202.resid_low, bf16[1024,768]{1,0:T(8,128)(2,1)} %bitcast.162, ...), custom_call_target="tpu_custom_call" | custom-call | flops 1 | bytes 1 | tf_op jit(solution)/shard_map/weight_sums/pallas_call | solution.py:707
  224.2 12.6 %weight_sums.3 = (f32[768,1920]{1,0:T(8,128)}, f32[1536,768]{1,0:T(8,128)}) custom-call(s32[1]{0:T(128)} %bitcast.32.meta, bf16[1024,768]{1,0:T(8,128)(2,1)} %get-tuple-element.201.second_in, bf16[1024,768]{1,0:T(8,128)(2,1)} %bitcast.160, bf16[1024,768]{1,0:T(8,128)(2,1)} %get-tuple-element.202.resid_low, bf16[1024,768]{1,0:T(8,128)(2,1)} %bitcast.163, ...), custom_call_target="tpu_custom_call" | custom-call | flops 1 | bytes 1 | tf_op jit(solution)/shard_map/weight_sums/pallas_call | solution.py:707
  247.8 5.6 %collective-permute-start.31 = (bf16[2,2,192,768]{3,2,0,1:T(8,128)(2,1)}, bf16[2,2,192,768]{3,2,0,1:T(8,128)(2,1)}, u32[]{:S(2)}, u32[]{:S(2)}) collective-permute-start(bf16[2,2,192,768]{3,2,0,1:T(8,128)(2,1)} %bitcast.152), channel_id=1, source_target_pairs={{0,8},{4,12},{8,0},{12,4},{16,24},{20,28},{24,16},{28,20},{1,9},{5... | collective-permute-start | bytes 3538952 | tf_op jit(solution)/shard_map/ppermute | solution.py:61
  255.9 41.3 %attend_back.2 = (f32[2,2304,256]{2,1,0:T(8,128)}, bf16[2,2304,256]{2,1,0:T(8,128)(2,1)}, f32[12,128]{1,0:T(8,128)}, f32[12,128]{1,0:T(8,128)}) custom-call(s32[3]{0:T(128)} %get-tuple-element.214.meta, bf16[256,2304]{1,0:T(8,128)(2,1)} %get-tuple-element.161.refs_0_, bf16[256,2304]{1,0:T(8,128)(2,1)} %collective-permute-done.8.refs_1_, ...), custom_call_target="tpu_custom_call" | custom-call | flops 60000002048 | bytes 1 | tf_op jit(solution)/shard_map/attend_back/pallas_call | solution.py:473
  314.7 14.6 %attend_back.3 = (f32[2,2304,256]{2,1,0:T(8,128)}, bf16[2,2304,256]{2,1,0:T(8,128)(2,1)}, f32[12,128]{1,0:T(8,128)}, f32[12,128]{1,0:T(8,128)}) custom-call(s32[3]{0:T(128)} %get-tuple-element.226.meta, bf16[256,2304]{1,0:T(8,128)(2,1)} %copy-done.13, bf16[256,2304]{1,0:T(8,128)(2,1)} %copy-done.20, bf16[256,2304]{1,0:T(8,128)(2,1)} %copy-done.21, ...), custom_call_target="tpu_custom_call" | custom-call | flops 1 | bytes 1 | tf_op jit(solution)/shard_map/attend_back/pallas_call | solution.py:473
  331.0 7.5 %collective-permute-done.34.far.refs_1_ = bf16[2304,256]{1,0:T(8,128)(2,1)S(1)} collective-permute-done((bf16[2304,256]{1,0:T(8,128)(2,1)}, bf16[2304,256]{1,0:T(8,128)(2,1)S(1)}, u32[]{:S(2)}, u32[]{:S(2)}) %collective-permute-start.34) | collective-permute-done | bytes 1179680 | tf_op jit(solution)/shard_map/ppermute | solution.py:61
  359.6 6.5 %token_grads.2 = (f32[4,256,768]{2,1,0:T(8,128)}, f32[8,768]{1,0:T(8,128)S(1)}) custom-call(s32[2]{0:T(128)S(1)} %compare_select_fusion.8.meta, f32[8,768]{1,0:T(8,128)S(1)} %get-tuple-element.167.gains, bf16[2304,256]{1,0:T(8,128)(2,1)S(1)} %get-tuple-element.367.near.refs_0_, bf16[2304,256]{1,0:T(8,128)(2,1)S(1)} %copy-done.7, ...), custom_call_target="tpu_custom_call" | custom-call | flops 1 | bytes 1 | tf_op jit(solution)/shard_map/token_grads/pallas_call | solution.py:993
  366.1 10.9 %collective-permute-done.40 = bf16[192,768]{1,0:T(8,128)(2,1)} collective-permute-done((bf16[192,768]{1,0:T(8,128)(2,1)}, bf16[192,768]{1,0:T(8,128)(2,1)}, u32[]{:S(2)}, u32[]{:S(2)}) %collective-permute-start.40) | collective-permute-done | bytes 294944 | tf_op jit(solution)/shard_map/ppermute | solution.py:61
  378.8 5.3 %collective-permute-done.39 = bf16[96,1920]{1,0:T(8,128)(2,1)} collective-permute-done((bf16[96,1920]{1,0:T(8,128)(2,1)}, bf16[96,1920]{1,0:T(8,128)(2,1)}, u32[]{:S(2)}, u32[]{:S(2)}) %collective-permute-start.39) | collective-permute-done | bytes 368672 | tf_op jit(solution)/shard_map/ppermute | solution.py:61
  386.0 5.3 %first_grads.2 = bf16[768,1152]{1,0:T(8,128)(2,1)} custom-call(s32[1]{0:T(128)} %bitcast.31.meta, bf16[1024,768]{1,0:T(8,128)(2,1)} %copy-done.10, bf16[2304,256]{1,0:T(8,128)(2,1)S(1)} %get-tuple-element.367.near.refs_0_, bf16[2304,256]{1,0:T(8,128)(2,1)S(1)} %copy-done.8, bf16[2304,256]{1,0:T(8,128)(2,1)S(1)} %copy-done.2, ...), custom_call_target="tpu_custom_call" | custom-call | flops 1 | bytes 1 | tf_op jit(solution)/shard_map/first_grads/pallas_call | solution.py:952
  395.1 5.8 %first_grads.3 = f32[768,1152]{1,0:T(8,128)} custom-call(s32[1]{0:T(128)} %bitcast.58.meta, bf16[1024,768]{1,0:T(8,128)(2,1)} %copy-done.10, bf16[2304,256]{1,0:T(8,128)(2,1)S(1)} %get-tuple-element.367.near.refs_0_, bf16[2304,256]{1,0:T(8,128)(2,1)S(1)} %copy-done.9, bf16[2304,256]{1,0:T(8,128)(2,1)S(1)} %copy-done.3, ...), custom_call_target="tpu_custom_call" | custom-call | flops 1 | bytes 1 | tf_op jit(solution)/shard_map/first_grads/pallas_call | solution.py:952
  417.8 7.1 %token_grads.3 = (f32[4,256,768]{2,1,0:T(8,128)}, f32[8,768]{1,0:T(8,128)S(1)}) custom-call(s32[2]{0:T(128)S(1)} %compare_select_fusion.9.meta, f32[8,768]{1,0:T(8,128)S(1)} %get-tuple-element.167.gains, bf16[2304,256]{1,0:T(8,128)(2,1)S(1)} %copy-done.4, bf16[2304,256]{1,0:T(8,128)(2,1)} %collective-permute-done.38.refs_3_.far, ...), custom_call_target="tpu_custom_call", output_to_operand_aliasing={{0}: (7, {})} | custom-call | flops 1 | bytes 1 | tf_op jit(solution)/shard_map/token_grads/pallas_call | solution.py:993
  431.8 7.6 %collective-permute-done.50 = bf16[2,96,768]{2,1,0:T(8,128)(2,1)S(1)} collective-permute-done((bf16[2,96,768]{2,1,0:T(8,128)(2,1)S(1)}, bf16[2,96,768]{2,1,0:T(8,128)(2,1)S(1)}, u32[]{:S(2)}, u32[]{:S(2)}) %collective-permute-start.50) | collective-permute-done | bytes 294944 | tf_op jit(solution)/shard_map/ppermute | solution.py:61
  450.0 6.5 %collective-permute-done.52 = bf16[96,1152]{1,0:T(8,128)(2,1)S(1)} collective-permute-done((bf16[96,1152]{1,0:T(8,128)(2,1)S(1)}, bf16[96,1152]{1,0:T(8,128)(2,1)S(1)}, u32[]{:S(2)}, u32[]{:S(2)}) %collective-permute-start.52) | collective-permute-done | bytes 221216 | tf_op jit(solution)/shard_map/ppermute | solution.py:61
  482.8 13.3 %adamw_all.1 = (f32[96,2304]{1,0:T(8,128)}, f32[96,2304]{1,0:T(8,128)}, f32[96,2304]{1,0:T(8,128)}, f32[96,2304]{1,0:T(8,128)}, f32[96,768]{1,0:T(8,128)}, /*ind...) custom-call(f32[1]{0:T(128)} %bitcast.80.factor, ...), custom_call_target="tpu_custom_call" | custom-call | tf_op jit(solution)/shard_map/adamw_all/pallas_call | solution.py:846
  (346 shorter events, 177.6 us)
Async XLA Ops:
  51.5 19.7 %collective-permute-start.8 = (bf16[256,2304]{1,0:T(8,128)(2,1)}, bf16[256,2304]{1,0:T(8,128)(2,1)}, u32[]{:S(2)}, u32[]{:S(2)}) collective-permute-start(bf16[256,2304]{1,0:T(8,128)(2,1)} %get-tuple-element.161.refs_0_), channel_id=1, source_target_pairs={{0,1},{1,0},{2,3},{3,2},{4,5},{5,4},{6,7},{7,6},{8,9},{9,8},{10,11... | collective-permute-start | bytes 3538952 | tf_op jit(solution)/shard_map/ppermute | solution.py:61
  51.7 28.6 %collective-permute-start.9 = (bf16[256,2304]{1,0:T(8,128)(2,1)}, bf16[256,2304]{1,0:T(8,128)(2,1)}, u32[]{:S(2)}, u32[]{:S(2)}) collective-permute-start(bf16[256,2304]{1,0:T(8,128)(2,1)} %get-tuple-element.170), channel_id=1, source_target_pairs={{0,2},{1,3},{2,0},{3,1},{4,6},{5,7},{6,4},{7,5},{8,10},{9,11},{10,... | collective-permute-start | bytes 3538952 | tf_op jit(solution)/shard_map/ppermute | solution.py:61
  61.5 32.7 %collective-permute-start.10 = (bf16[1,96,3456]{2,1,0:T(8,128)(2,1)S(1)}, bf16[1,96,3456]{2,1,0:T(8,128)(2,1)}, u32[]{:S(2)}, u32[]{:S(2)}) collective-permute-start(bf16[1,96,3456]{2,1,0:T(8,128)(2,1)S(1)} %bitcast.156), channel_id=1, source_target_pairs={{0,16},{4,20},{8,24},{12,28},{16,0},{20,4},{24,8},{28,12},{1,17},{... | collective-permute-start | bytes 1990664 | tf_op jit(solution)/shard_map/ppermute | solution.py:61
  95.5 31.7 %collective-permute-start.12 = (bf16[2,96,3456]{2,1,0:T(8,128)(2,1)S(1)}, bf16[2,96,3456]{2,1,0:T(8,128)(2,1)}, u32[]{:S(2)}, u32[]{:S(2)}) collective-permute-start(bf16[2,96,3456]{2,1,0:T(8,128)(2,1)S(1)} %pad_maximum_fusion.1.refs_0_), channel_id=1, source_target_pairs={{0,8},{4,12},{8,0},{12,4},{16,24},{20,28},{24,16},{28,20},{1,9},{5... | collective-permute-start | bytes 3981320 | tf_op jit(solution)/shard_map/ppermute | solution.py:61
  96.2 31.4 %collective-permute-start.13 = (bf16[2,96,3456]{2,1,0:T(8,128)(2,1)S(1)}, bf16[2,96,3456]{2,1,0:T(8,128)(2,1)}, u32[]{:S(2)}, u32[]{:S(2)}) collective-permute-start(bf16[2,96,3456]{2,1,0:T(8,128)(2,1)S(1)} %pad_maximum_fusion.1.refs_0_), channel_id=1, source_target_pairs={{0,4},{4,0},{8,12},{12,8},{16,20},{20,16},{24,28},{28,24},{1,5},{5... | collective-permute-start | bytes 3981320 | tf_op jit(solution)/shard_map/ppermute | solution.py:61
  97.6 29.9 %collective-permute-start.16 = (bf16[2,96,3456]{2,1,0:T(8,128)(2,1)S(1)}, bf16[2,96,3456]{2,1,0:T(8,128)(2,1)S(1)}, u32[]{:S(2)}, u32[]{:S(2)}) collective-permute-start(bf16[2,96,3456]{2,1,0:T(8,128)(2,1)S(1)} %pad_maximum_fusion.1.refs_0_), channel_id=1, source_target_pairs={{0,1},{1,0},{2,3},{3,2},{4,5},{5,4},{6,7},{7,6},{8,9},{9,8},{10,11... | collective-permute-start | bytes 3981320 | tf_op jit(solution)/shard_map/ppermute | solution.py:61
  97.6 26.0 %collective-permute-start.15 = (bf16[256,2304]{1,0:T(8,128)(2,1)S(1)}, bf16[256,2304]{1,0:T(8,128)(2,1)S(1)}, u32[]{:S(2)}, u32[]{:S(2)}) collective-permute-start(bf16[256,2304]{1,0:T(8,128)(2,1)S(1)} %get-tuple-element.184.refs_0_), channel_id=1, source_target_pairs={{0,1},{1,0},{2,3},{3,2},{4,5},{5,4},{6,7},{7,6},{8,9},{9,8},{10,11... | collective-permute-start | bytes 3538952 | tf_op jit(solution)/shard_map/ppermute | solution.py:61
  98.2 27.9 %collective-permute-start.14 = (bf16[256,2304]{1,0:T(8,128)(2,1)S(1)}, bf16[256,2304]{1,0:T(8,128)(2,1)S(1)}, u32[]{:S(2)}, u32[]{:S(2)}) collective-permute-start(bf16[256,2304]{1,0:T(8,128)(2,1)S(1)} %get-tuple-element.183), channel_id=1, source_target_pairs={{0,2},{1,3},{2,0},{3,1},{4,6},{5,7},{6,4},{7,5},{8,10},{9,11},{10,... | collective-permute-start | bytes 3538952 | tf_op jit(solution)/shard_map/ppermute | solution.py:61
  128.9 22.4 %collective-permute-start.18 = (bf16[2,128,768]{2,1,0:T(8,128)(2,1)S(1)}, bf16[2,128,768]{2,1,0:T(8,128)(2,1)S(1)}, u32[]{:S(2)}, u32[]{:S(2)}) collective-permute-start(bf16[2,128,768]{2,1,0:T(8,128)(2,1)S(1)} %slice.142), channel_id=1, source_target_pairs={{0,2},{1,3},{2,0},{3,1},{4,6},{5,7},{6,4},{7,5},{8,10},{9,11},{10,... | collective-permute-start | bytes 1179656 | tf_op jit(solution)/shard_map/ppermute | solution.py:61
  129.4 31.9 %collective-permute-start.21 = (bf16[2,96,3456]{2,1,0:T(8,128)(2,1)}, bf16[2,96,3456]{2,1,0:T(8,128)(2,1)}, u32[]{:S(2)}, u32[]{:S(2)}) collective-permute-start(bf16[2,96,3456]{2,1,0:T(8,128)(2,1)} %collective-permute-done.12.refs_1_), channel_id=1, source_target_pairs={{0,4},{4,0},{8,12},{12,8},{16,20},{20,16},{24,28},{28,24},{1,5},{5... | collective-permute-start | bytes 3981320 | tf_op jit(solution)/shard_map/ppermute | solution.py:61
  130.9 30.4 %collective-permute-start.22 = (bf16[2,96,3456]{2,1,0:T(8,128)(2,1)}, bf16[2,96,3456]{2,1,0:T(8,128)(2,1)}, u32[]{:S(2)}, u32[]{:S(2)}) collective-permute-start(bf16[2,96,3456]{2,1,0:T(8,128)(2,1)} %collective-permute-done.12.refs_1_), channel_id=1, source_target_pairs={{0,1},{1,0},{2,3},{3,2},{4,5},{5,4},{6,7},{7,6},{8,9},{9,8},{10,11... | collective-permute-start | bytes 3981320 | tf_op jit(solution)/shard_map/ppermute | solution.py:61
  130.9 30.4 %collective-permute-start.23 = (bf16[2,96,3456]{2,1,0:T(8,128)(2,1)}, bf16[2,96,3456]{2,1,0:T(8,128)(2,1)}, u32[]{:S(2)}, u32[]{:S(2)}) collective-permute-start(bf16[2,96,3456]{2,1,0:T(8,128)(2,1)} %collective-permute-done.13.refs_2_), channel_id=1, source_target_pairs={{0,1},{1,0},{2,3},{3,2},{4,5},{5,4},{6,7},{7,6},{8,9},{9,8},{10,11... | collective-permute-start | bytes 3981320 | tf_op jit(solution)/shard_map/ppermute | solution.py:61
  221.6 18.2 %collective-permute-start.25 = (bf16[768,1920]{1,0:T(8,128)(2,1)}, bf16[768,1920]{1,0:T(8,128)(2,1)}, u32[]{:S(2)}, u32[]{:S(2)}) collective-permute-start(bf16[768,1920]{1,0:T(8,128)(2,1)} %get-tuple-element.205), channel_id=1, source_target_pairs={{0,1},{1,0},{2,3},{3,2},{4,5},{5,4},{6,7},{7,6},{8,9},{9,8},{10,11... | collective-permute-start | bytes 8847368 | tf_op jit(solution)/shard_map/ppermute | solution.py:61
  221.8 18.0 %collective-permute-start.26 = (bf16[1536,768]{1,0:T(8,128)(2,1)}, bf16[1536,768]{1,0:T(8,128)(2,1)}, u32[]{:S(2)}, u32[]{:S(2)}) collective-permute-start(bf16[1536,768]{1,0:T(8,128)(2,1)} %get-tuple-element.206), channel_id=1, source_target_pairs={{0,1},{1,0},{2,3},{3,2},{4,5},{5,4},{6,7},{7,6},{8,9},{9,8},{10,11... | collective-permute-start | bytes 7077896 | tf_op jit(solution)/shard_map/ppermute | solution.py:61
  238.0 65.1 %collective-permute-start.29 = (bf16[2,128,768]{2,1,0:T(8,128)(2,1)}, bf16[2,128,768]{2,1,0:T(8,128)(2,1)}, u32[]{:S(2)}, u32[]{:S(2)}) collective-permute-start(bf16[2,128,768]{2,1,0:T(8,128)(2,1)} %slice_bitcast_fusion.4), channel_id=1, source_target_pairs={{0,2},{1,3},{2,0},{3,1},{4,6},{5,7},{6,4},{7,5},{8,10},{9,11},{10,... | collective-permute-start | bytes 1179656 | tf_op jit(solution)/shard_map/ppermute | solution.py:61
  247.8 49.5 %collective-permute-start.31 = (bf16[2,2,192,768]{3,2,0,1:T(8,128)(2,1)}, bf16[2,2,192,768]{3,2,0,1:T(8,128)(2,1)}, u32[]{:S(2)}, u32[]{:S(2)}) collective-permute-start(bf16[2,2,192,768]{3,2,0,1:T(8,128)(2,1)} %bitcast.152), channel_id=1, source_target_pairs={{0,8},{4,12},{8,0},{12,4},{16,24},{20,28},{24,16},{28,20},{1,9},{5... | collective-permute-start | bytes 3538952 | tf_op jit(solution)/shard_map/ppermute | solution.py:61
  253.4 46.6 %collective-permute-start.30 = (bf16[2,2,96,1920]{3,2,0,1:T(8,128)(2,1)}, bf16[2,2,96,1920]{3,2,0,1:T(8,128)(2,1)}, u32[]{:S(2)}, u32[]{:S(2)}) collective-permute-start(bf16[2,2,96,1920]{3,2,0,1:T(8,128)(2,1)} %bitcast.151), channel_id=1, source_target_pairs={{0,4},{4,0},{8,12},{12,8},{16,20},{20,16},{24,28},{28,24},{1,5},{5... | collective-permute-start | bytes 4423688 | tf_op jit(solution)/shard_map/ppermute | solution.py:61
  310.3 28.2 %collective-permute-start.34 = (bf16[2304,256]{1,0:T(8,128)(2,1)}, bf16[2304,256]{1,0:T(8,128)(2,1)S(1)}, u32[]{:S(2)}, u32[]{:S(2)}) collective-permute-start(bf16[2304,256]{1,0:T(8,128)(2,1)} %get-tuple-element.366), channel_id=1, source_target_pairs={{0,2},{1,3},{2,0},{3,1},{4,6},{5,7},{6,4},{7,5},{8,10},{9,11},{10,... | collective-permute-start | bytes 3538952 | tf_op jit(solution)/shard_map/ppermute | solution.py:61
  311.7 19.4 %collective-permute-start.35 = (bf16[2,96,1920]{2,1,0:T(8,128)(2,1)}, bf16[2,96,1920]{2,1,0:T(8,128)(2,1)}, u32[]{:S(2)}, u32[]{:S(2)}) collective-permute-start(bf16[2,96,1920]{2,1,0:T(8,128)(2,1)} %get-tuple-element.376), channel_id=1, source_target_pairs={{0,8},{4,12},{8,0},{12,4},{16,24},{20,28},{24,16},{28,20},{1,9},{5... | collective-permute-start | bytes 2211848 | tf_op jit(solution)/shard_map/ppermute | solution.py:61
  351.7 25.3 %collective-permute-start.40 = (bf16[192,768]{1,0:T(8,128)(2,1)}, bf16[192,768]{1,0:T(8,128)(2,1)}, u32[]{:S(2)}, u32[]{:S(2)}) collective-permute-start(bf16[192,768]{1,0:T(8,128)(2,1)} %dynamic-slice_bitcast_fusion.6), channel_id=1, source_target_pairs={{0,16},{4,20},{8,24},{12,28},{16,0},{20,4},{24,8},{28,12},{1,17},{... | collective-permute-start | bytes 884744 | tf_op jit(solution)/shard_map/ppermute | solution.py:61
  352.2 33.8 %collective-permute-start.38 = (bf16[2304,256]{1,0:T(8,128)(2,1)}, bf16[2304,256]{1,0:T(8,128)(2,1)}, u32[]{:S(2)}, u32[]{:S(2)}) collective-permute-start(bf16[2304,256]{1,0:T(8,128)(2,1)} %get-tuple-element.364), channel_id=1, source_target_pairs={{0,2},{1,3},{2,0},{3,1},{4,6},{5,7},{6,4},{7,5},{8,10},{9,11},{10,... | collective-permute-start | bytes 3538952 | tf_op jit(solution)/shard_map/ppermute | solution.py:61
  354.8 29.3 %collective-permute-start.39 = (bf16[96,1920]{1,0:T(8,128)(2,1)}, bf16[96,1920]{1,0:T(8,128)(2,1)}, u32[]{:S(2)}, u32[]{:S(2)}) collective-permute-start(bf16[96,1920]{1,0:T(8,128)(2,1)} %dynamic-slice_bitcast_fusion.4), channel_id=1, source_target_pairs={{0,16},{4,20},{8,24},{12,28},{16,0},{20,4},{24,8},{28,12},{1,17},{... | collective-permute-start | bytes 1105928 | tf_op jit(solution)/shard_map/ppermute | solution.py:61
  407.0 21.2 %collective-permute-start.49 = (bf16[2,2,96,768]{3,2,0,1:T(8,128)(2,1)S(1)}, bf16[2,2,96,768]{3,2,0,1:T(8,128)(2,1)S(1)}, u32[]{:S(2)}, u32[]{:S(2)}) collective-permute-start(bf16[2,2,96,768]{3,2,0,1:T(8,128)(2,1)S(1)} %bitcast.182), channel_id=1, source_target_pairs={{0,4},{4,0},{8,12},{12,8},{16,20},{20,16},{24,28},{28,24},{1,5},{5... | collective-permute-start | bytes 1769480 | tf_op jit(solution)/shard_map/ppermute | solution.py:61
  426.2 23.8 %collective-permute-start.54 = (f32[16,128]{1,0:T(8,128)S(1)}, f32[16,128]{1,0:T(8,128)S(1)}, u32[]{:S(2)}, u32[]{:S(2)}) collective-permute-start(f32[16,128]{1,0:T(8,128)S(1)} %fusion.35), channel_id=1, source_target_pairs={{0,2},{1,3},{2,0},{3,1},{4,6},{5,7},{6,4},{7,5},{8,10},{9,11},{10,... | collective-permute-start | bytes 24584 | tf_op jit(solution)/shard_map/ppermute | solution.py:61
  (89 other events, 838.0 us)
where the time goes:
time: 503 us; the launch traced here: 498 us
  Pallas kernels  218 us (43%)
  waiting for transfers between devices  112 us (22%)
  starting transfers between devices  66 us (13%)
  local copies, waits for them, and re-layouts  42.3 us (8%)
  other arithmetic  39.2 us (8%)
  between operations  19.5 us (4%)
    ppermute x63, waiting for transfers between devices, swap(): return lax.ppermute(value, axis, [(i, i ^ mask) for i in range(size)])  112 us
    ppermute x63, starting transfers between devices, swap(): return lax.ppermute(value, axis, [(i, i ^ mask) for i in range(size)])  66 us
    pallas_call x2, Pallas kernels, attend_back(): pl.pallas_call(backward_kernel, grid_spec=pltpu.PrefetchScalarGridSpec(nu...  56 us
    pallas_call x1, Pallas kernels, feed_forward(): pl.pallas_call(partial(feed_kernel, offs), grid_spec=pltpu.PrefetchScalar...  43.9 us
    pallas_call x2, Pallas kernels, attend(): pl.pallas_call(forward_kernel, grid_spec=pltpu.PrefetchScalarGridSpec(num...  41 us
    pallas_call x2, Pallas kernels, weight_sums(): pl.pallas_call(weight_kernel, grid_spec=pltpu.PrefetchScalarGridSpec(num_...  24.1 us
    unnamed x107, local copies, waits for them, and re-layouts  21.7 us
    pallas_call x2, Pallas kernels, token_grads(): pl.pallas_call(token_grads_kernel, grid_spec=pltpu.PrefetchScalarGridSpec...  13.5 us
  transfers between devices with their start and end apart: 63, of which 25 were waited for; matrix products, arithmetic and copies ran while one was open for 9% of the time, Pallas kernels for 28%

commit v1 on v0

--- a/solution.py
+++ b/solution.py
@@ -1201,6 +1201,8 @@
     place, beside, mixers, metas, grad_out = lax.optimization_barrier(
         (place, beside, mixers, metas, grad_out)
     )
+    if offs is not None:
+        place, got = lax.optimization_barrier((place, got))
     pre_mix, post_mix, pre_back, post_back = mixers
     *out, first_in, gain_vals, weight_qkv = first_product(
         place, tokens, pieces, offs, (2, 3), 4, True
@@ -1209,7 +1211,6 @@
     far.append(out[1])
     here = after(here, far[1], near[1])
     if offs is not None:
-        here, got = lax.optimization_barrier((here, got))
         rest_pieces = [jnp.concatenate([rest, got])]
         far_z, far_x = swap(rest_pieces[0], "dp", 2), swap(rest_pieces[0], "dp", 1)
     sources = [[near[0], beside, here, swap(here, "seq", 1)]]

time: 503 us -> 514 us (1.022)
  Pallas kernels: 218 us -> 229 us
  waiting for transfers between devices: 112 us -> 104 us
    ppermute x63, waiting for transfers between devices: 112 us -> 104 us  [swap(): return lax.ppermute(value, axis, [(i, i ^ mask) for i in range(size)])]
    pallas_call x2, Pallas kernels: 56 us -> 62.6 us  [attend_back(): pl.pallas_call(backward_kernel, grid_spec=pltpu.PrefetchScalarGridSpec(nu...]
    ppermute x63, starting transfers between devices: 66 us -> 71.1 us  [swap(): return lax.ppermute(value, axis, [(i, i ^ mask) for i in range(size)])]
  transfers between devices with their start and end apart: 63 -> 63, of which waited for: 25 -> 25; matrix products, arithmetic and copies ran while one was open for 9% -> 9% of each run, Pallas kernels for 28% -> 29%
where the time goes in v1:
time: 514 us; the launch traced here: 507 us
  Pallas kernels  229 us (45%)
  waiting for transfers between devices  104 us (20%)
  starting transfers between devices  71.1 us (14%)
  local copies, waits for them, and re-layouts  43 us (8%)
  other arithmetic  39.6 us (8%)
  between operations  19.5 us (4%)
    ppermute x63, waiting for transfers between devices, swap(): return lax.ppermute(value, axis, [(i, i ^ mask) for i in range(size)])  104 us
    ppermute x63, starting transfers between devices, swap(): return lax.ppermute(value, axis, [(i, i ^ mask) for i in range(size)])  71.1 us
    pallas_call x2, Pallas kernels, attend_back(): pl.pallas_call(backward_kernel, grid_spec=pltpu.PrefetchScalarGridSpec(nu...  62.6 us
    pallas_call x2, Pallas kernels, attend(): pl.pallas_call(forward_kernel, grid_spec=pltpu.PrefetchScalarGridSpec(num...  45.1 us
    pallas_call x1, Pallas kernels, feed_forward(): pl.pallas_call(partial(feed_kernel, offs), grid_spec=pltpu.PrefetchScalar...  43.9 us
    pallas_call x2, Pallas kernels, weight_sums(): pl.pallas_call(weight_kernel, grid_spec=pltpu.PrefetchScalarGridSpec(num_...  24.1 us
    unnamed x107, local copies, waits for them, and re-layouts  22.4 us
    pallas_call x2, Pallas kernels, token_grads(): pl.pallas_call(token_grads_kernel, grid_spec=pltpu.PrefetchScalarGridSpec...  13.5 us
  transfers between devices with their start and end apart: 63, of which 25 were waited for; matrix products, arithmetic and copies ran while one was open for 9% of the time, Pallas kernels for 29%

profile of v1, /device:TPU:0, one launch (start us, length us, event | category | flops | bytes accessed | tf_op | source)
XLA Modules:
  0.0 506.6 jit_solution(11484714649418893276)
XLA Ops:
  21.5 9.6 %collective-permute-done.1.refs_1_ = bf16[2,96,1280]{2,1,0:T(8,128)(2,1)S(1)} collective-permute-done((bf16[2,96,1280]{2,1,0:T(8,128)(2,1)S(1)}, bf16[2,96,1280]{2,1,0:T(8,128)(2,1)S(1)}, u32[]{:S(2)}, u32[]{:S(2)}) %collective-permute-start.1) | collective-permute-done | bytes 491552 | tf_op jit(solution)/shard_map/ppermute | solution.py:61
  33.1 10.0 %collective-permute-done.3.refs_3_ = bf16[2,96,1280]{2,1,0:T(8,128)(2,1)} collective-permute-done((bf16[2,96,1280]{2,1,0:T(8,128)(2,1)S(1)}, bf16[2,96,1280]{2,1,0:T(8,128)(2,1)}, u32[]{:S(2)}, u32[]{:S(2)}) %collective-permute-start.3) | collective-permute-done | bytes 491552 | tf_op jit(solution)/shard_map/ppermute | solution.py:61
  45.3 6.2 %first_product.2 = (bf16[256,2304]{1,0:T(8,128)(2,1)}, bf16[256,2304]{1,0:T(8,128)(2,1)}, bf16[512,768]{1,0:T(8,128)(2,1)}, f32[8,768]{1,0:T(8,128)}) custom-call(s32[6]{0:T(128)S(1)} %compare_select_fusion.5.meta, bf16[4,256,768]{2,1,0:T(8,128)(2,1)S(1)} %copy-done, bf16[2,96,1280]{2,1,0:T(8,128)(2,1)S(1)} %pad_maximum_fusion.7.refs_0_, ...), custom_call_target="tpu_custom_call" | custom-call | flops 1 | bytes 1 | tf_op jit(solution)/shard_map/first_product/pallas_call | solution.py:920
  71.2 23.1 %collective-permute-done.9 = bf16[1,96,3456]{2,1,0:T(8,128)(2,1)} collective-permute-done((bf16[1,96,3456]{2,1,0:T(8,128)(2,1)S(1)}, bf16[1,96,3456]{2,1,0:T(8,128)(2,1)}, u32[]{:S(2)}, u32[]{:S(2)}) %collective-permute-start.9) | collective-permute-done | bytes 663584 | tf_op jit(solution)/shard_map/ppermute | solution.py:61
  94.3 5.3 %first_product.3 = (bf16[256,2304]{1,0:T(8,128)(2,1)S(1)}, bf16[256,2304]{1,0:T(8,128)(2,1)S(1)}, bf16[1024,768]{1,0:T(8,128)(2,1)S(1)}, f32[8,768]{1,0:T(8,128)S(1)}, bf16[768,2304]{1,0:T(8,128)(2,1)S(1)}) custom-call(s32[6]{0:T(128)S(1)} %compare_select_fusion.5.meta, bf16[4,256,768]{2,1,0:T(8,128)(2,1)S(1)} %copy-done, ...), custom_call_target="tpu_custom_call" | custom-call | flops 1 | bytes 1 | tf_op jit(solution)/shard_map/first_product/pallas_call | solution.py:920
  107.4 24.9 %attend.2 = (bf16[4,128,768]{2,1,0:T(8,128)(2,1)}, bf16[5,12,128,1024]{3,2,1,0:T(8,128)(2,1)}, bf16[5,12,128,1024]{3,2,1,0:T(8,128)(2,1)}) custom-call(s32[3]{0:T(128)} %get-tuple-element.214.meta, bf16[256,2304]{1,0:T(8,128)(2,1)} %get-tuple-element.161.refs_0_, bf16[256,2304]{1,0:T(8,128)(2,1)} %collective-permute-done.8.refs_1_, ...), custom_call_target="tpu_custom_call" | custom-call | flops 60000002048 | bytes 1 | tf_op jit(solution)/shard_map/attend/pallas_call | solution.py:427
  140.8 20.2 %attend.3 = (bf16[4,128,768]{2,1,0:T(8,128)(2,1)}, bf16[5,12,128,1024]{3,2,1,0:T(8,128)(2,1)}, bf16[5,12,128,1024]{3,2,1,0:T(8,128)(2,1)}) custom-call(s32[3]{0:T(128)} %get-tuple-element.226.meta, bf16[256,2304]{1,0:T(8,128)(2,1)} %copy-done.13, bf16[256,2304]{1,0:T(8,128)(2,1)} %copy-done.20, bf16[256,2304]{1,0:T(8,128)(2,1)} %copy-done.21, ...), custom_call_target="tpu_custom_call" | custom-call | flops 1 | bytes 1 | tf_op jit(solution)/shard_map/attend/pallas_call | solution.py:427
  162.1 5.0 collective-permute-start.19
  167.3 9.1 %collective-permute-done.19 = bf16[2,128,768]{2,1,0:T(8,128)(2,1)S(1)} collective-permute-done((bf16[2,128,768]{2,1,0:T(8,128)(2,1)S(1)}, bf16[2,128,768]{2,1,0:T(8,128)(2,1)S(1)}, u32[]{:S(2)}, u32[]{:S(2)}) %collective-permute-start.19) | collective-permute-done | bytes 393248 | tf_op jit(solution)/shard_map/ppermute | solution.py:61
  182.1 43.9 %feed_forward.1 = (bf16[1024,768]{1,0:T(8,128)(2,1)}, f32[1024,768]{1,0:T(8,128)}, bf16[1024,768]{1,0:T(8,128)(2,1)}, bf16[1024,768]{1,0:T(8,128)(2,1)}, f32[8,7...) custom-call(s32[6]{0:T(128)} %copy-done.18, ...), custom_call_target="tpu_custom_call" | custom-call | flops 22000001024 | bytes 40000000 | tf_op jit(solution)/shard_map/feed_forward/pallas_call | solution.py:644
  226.1 11.5 %weight_sums.2 = (bf16[768,1920]{1,0:T(8,128)(2,1)}, bf16[1536,768]{1,0:T(8,128)(2,1)}) custom-call(s32[1]{0:T(128)} %bitcast.31.meta, bf16[1024,768]{1,0:T(8,128)(2,1)} %get-tuple-element.201.second_in, bf16[1024,768]{1,0:T(8,128)(2,1)} %bitcast.159, bf16[1024,768]{1,0:T(8,128)(2,1)} %get-tuple-element.202.resid_low, bf16[1024,768]{1,0:T(8,128)(2,1)} %bitcast.162, ...), custom_call_target="tpu_custom_call" | custom-call | flops 1 | bytes 1 | tf_op jit(solution)/shard_map/weight_sums/pallas_call | solution.py:707
  240.1 12.6 %weight_sums.3 = (f32[768,1920]{1,0:T(8,128)}, f32[1536,768]{1,0:T(8,128)}) custom-call(s32[1]{0:T(128)} %bitcast.32.meta, bf16[1024,768]{1,0:T(8,128)(2,1)} %get-tuple-element.201.second_in, bf16[1024,768]{1,0:T(8,128)(2,1)} %bitcast.160, bf16[1024,768]{1,0:T(8,128)(2,1)} %get-tuple-element.202.resid_low, bf16[1024,768]{1,0:T(8,128)(2,1)} %bitcast.163, ...), custom_call_target="tpu_custom_call" | custom-call | flops 1 | bytes 1 | tf_op jit(solution)/shard_map/weight_sums/pallas_call | solution.py:707
  263.7 41.3 %attend_back.2 = (f32[2,2304,256]{2,1,0:T(8,128)}, bf16[2,2304,256]{2,1,0:T(8,128)(2,1)}, f32[12,128]{1,0:T(8,128)}, f32[12,128]{1,0:T(8,128)}) custom-call(s32[3]{0:T(128)} %get-tuple-element.214.meta, bf16[256,2304]{1,0:T(8,128)(2,1)} %get-tuple-element.161.refs_0_, bf16[256,2304]{1,0:T(8,128)(2,1)} %collective-permute-done.8.refs_1_, ...), custom_call_target="tpu_custom_call" | custom-call | flops 60000002048 | bytes 1 | tf_op jit(solution)/shard_map/attend_back/pallas_call | solution.py:473
  324.5 21.2 %attend_back.3 = (f32[2,2304,256]{2,1,0:T(8,128)}, bf16[2,2304,256]{2,1,0:T(8,128)(2,1)}, f32[12,128]{1,0:T(8,128)}, f32[12,128]{1,0:T(8,128)}) custom-call(s32[3]{0:T(128)} %get-tuple-element.226.meta, bf16[256,2304]{1,0:T(8,128)(2,1)} %copy-done.13, bf16[256,2304]{1,0:T(8,128)(2,1)} %copy-done.20, bf16[256,2304]{1,0:T(8,128)(2,1)} %copy-done.21, ...), custom_call_target="tpu_custom_call" | custom-call | flops 1 | bytes 1 | tf_op jit(solution)/shard_map/attend_back/pallas_call | solution.py:473
  347.5 4.9 collective-permute-done.37
  359.9 10.2 %collective-permute-start.38 = (bf16[2304,256]{1,0:T(8,128)(2,1)}, bf16[2304,256]{1,0:T(8,128)(2,1)}, u32[]{:S(2)}, u32[]{:S(2)}) collective-permute-start(bf16[2304,256]{1,0:T(8,128)(2,1)} %get-tuple-element.364), channel_id=1, source_target_pairs={{0,2},{1,3},{2,0},{3,1},{4,6},{5,7},{6,4},{7,5},{8,10},{9,11},{10,... | collective-permute-start | bytes 3538952 | tf_op jit(solution)/shard_map/ppermute | solution.py:61
  377.7 6.5 %token_grads.2 = (f32[4,256,768]{2,1,0:T(8,128)}, f32[8,768]{1,0:T(8,128)S(1)}) custom-call(s32[2]{0:T(128)S(1)} %compare_select_fusion.8.meta, f32[8,768]{1,0:T(8,128)S(1)} %get-tuple-element.169.gains, bf16[2304,256]{1,0:T(8,128)(2,1)S(1)} %get-tuple-element.367.near.refs_0_, bf16[2304,256]{1,0:T(8,128)(2,1)S(1)} %copy-done.7, ...), custom_call_target="tpu_custom_call" | custom-call | flops 1 | bytes 1 | tf_op jit(solution)/shard_map/token_grads/pallas_call | solution.py:993
  386.7 5.3 %collective-permute-done.39 = bf16[96,1920]{1,0:T(8,128)(2,1)} collective-permute-done((bf16[96,1920]{1,0:T(8,128)(2,1)}, bf16[96,1920]{1,0:T(8,128)(2,1)}, u32[]{:S(2)}, u32[]{:S(2)}) %collective-permute-start.39) | collective-permute-done | bytes 368672 | tf_op jit(solution)/shard_map/ppermute | solution.py:61
  396.7 5.3 %first_grads.2 = bf16[768,1152]{1,0:T(8,128)(2,1)} custom-call(s32[1]{0:T(128)} %bitcast.31.meta, bf16[1024,768]{1,0:T(8,128)(2,1)} %copy-done.10, bf16[2304,256]{1,0:T(8,128)(2,1)S(1)} %get-tuple-element.367.near.refs_0_, bf16[2304,256]{1,0:T(8,128)(2,1)S(1)} %copy-done.8, bf16[2304,256]{1,0:T(8,128)(2,1)S(1)} %copy-done.2, ...), custom_call_target="tpu_custom_call" | custom-call | flops 1 | bytes 1 | tf_op jit(solution)/shard_map/first_grads/pallas_call | solution.py:952
  405.9 5.8 %first_grads.3 = f32[768,1152]{1,0:T(8,128)} custom-call(s32[1]{0:T(128)} %bitcast.58.meta, bf16[1024,768]{1,0:T(8,128)(2,1)} %copy-done.10, bf16[2304,256]{1,0:T(8,128)(2,1)S(1)} %get-tuple-element.367.near.refs_0_, bf16[2304,256]{1,0:T(8,128)(2,1)S(1)} %copy-done.9, bf16[2304,256]{1,0:T(8,128)(2,1)S(1)} %copy-done.3, ...), custom_call_target="tpu_custom_call" | custom-call | flops 1 | bytes 1 | tf_op jit(solution)/shard_map/first_grads/pallas_call | solution.py:952
  420.5 4.9 collective-permute-done.42
  425.7 7.1 %token_grads.3 = (f32[4,256,768]{2,1,0:T(8,128)}, f32[8,768]{1,0:T(8,128)S(1)}) custom-call(s32[2]{0:T(128)S(1)} %compare_select_fusion.9.meta, f32[8,768]{1,0:T(8,128)S(1)} %get-tuple-element.169.gains, bf16[2304,256]{1,0:T(8,128)(2,1)S(1)} %copy-done.4, bf16[2304,256]{1,0:T(8,128)(2,1)} %collective-permute-done.38.refs_3_.far, ...), custom_call_target="tpu_custom_call", output_to_operand_aliasing={{0}: (7, {})} | custom-call | flops 1 | bytes 1 | tf_op jit(solution)/shard_map/token_grads/pallas_call | solution.py:993
  440.7 6.6 %collective-permute-done.50 = bf16[2,96,768]{2,1,0:T(8,128)(2,1)S(1)} collective-permute-done((bf16[2,96,768]{2,1,0:T(8,128)(2,1)S(1)}, bf16[2,96,768]{2,1,0:T(8,128)(2,1)S(1)}, u32[]{:S(2)}, u32[]{:S(2)}) %collective-permute-start.50) | collective-permute-done | bytes 294944 | tf_op jit(solution)/shard_map/ppermute | solution.py:61
  491.7 13.3 %adamw_all.1 = (f32[96,2304]{1,0:T(8,128)}, f32[96,2304]{1,0:T(8,128)}, f32[96,2304]{1,0:T(8,128)}, f32[96,2304]{1,0:T(8,128)}, f32[96,768]{1,0:T(8,128)}, /*ind...) custom-call(f32[1]{0:T(128)} %bitcast.80.factor, ...), custom_call_target="tpu_custom_call" | custom-call | tf_op jit(solution)/shard_map/adamw_all/pallas_call | solution.py:846
  (346 shorter events, 173.2 us)
Async XLA Ops:
  51.5 19.7 %collective-permute-start.8 = (bf16[256,2304]{1,0:T(8,128)(2,1)}, bf16[256,2304]{1,0:T(8,128)(2,1)}, u32[]{:S(2)}, u32[]{:S(2)}) collective-permute-start(bf16[256,2304]{1,0:T(8,128)(2,1)} %get-tuple-element.161.refs_0_), channel_id=1, source_target_pairs={{0,1},{1,0},{2,3},{3,2},{4,5},{5,4},{6,7},{7,6},{8,9},{9,8},{10,11... | collective-permute-start | bytes 3538952 | tf_op jit(solution)/shard_map/ppermute | solution.py:61
  51.7 50.9 %collective-permute-start.10 = (bf16[256,2304]{1,0:T(8,128)(2,1)}, bf16[256,2304]{1,0:T(8,128)(2,1)}, u32[]{:S(2)}, u32[]{:S(2)}) collective-permute-start(bf16[256,2304]{1,0:T(8,128)(2,1)} %get-tuple-element.172), channel_id=1, source_target_pairs={{0,2},{1,3},{2,0},{3,1},{4,6},{5,7},{6,4},{7,5},{8,10},{9,11},{10,... | collective-permute-start | bytes 3538952 | tf_op jit(solution)/shard_map/ppermute | solution.py:61
  61.5 32.7 %collective-permute-start.9 = (bf16[1,96,3456]{2,1,0:T(8,128)(2,1)S(1)}, bf16[1,96,3456]{2,1,0:T(8,128)(2,1)}, u32[]{:S(2)}, u32[]{:S(2)}) collective-permute-start(bf16[1,96,3456]{2,1,0:T(8,128)(2,1)S(1)} %bitcast.156), channel_id=1, source_target_pairs={{0,16},{4,20},{8,24},{12,28},{16,0},{20,4},{24,8},{28,12},{1,17},{... | collective-permute-start | bytes 1990664 | tf_op jit(solution)/shard_map/ppermute | solution.py:61
  104.3 31.3 %collective-permute-start.12 = (bf16[2,96,3456]{2,1,0:T(8,128)(2,1)S(1)}, bf16[2,96,3456]{2,1,0:T(8,128)(2,1)}, u32[]{:S(2)}, u32[]{:S(2)}) collective-permute-start(bf16[2,96,3456]{2,1,0:T(8,128)(2,1)S(1)} %pad_maximum_fusion.1.refs_0_), channel_id=1, source_target_pairs={{0,8},{4,12},{8,0},{12,4},{16,24},{20,28},{24,16},{28,20},{1,9},{5... | collective-permute-start | bytes 3981320 | tf_op jit(solution)/shard_map/ppermute | solution.py:61
  104.9 30.9 %collective-permute-start.13 = (bf16[2,96,3456]{2,1,0:T(8,128)(2,1)S(1)}, bf16[2,96,3456]{2,1,0:T(8,128)(2,1)}, u32[]{:S(2)}, u32[]{:S(2)}) collective-permute-start(bf16[2,96,3456]{2,1,0:T(8,128)(2,1)S(1)} %pad_maximum_fusion.1.refs_0_), channel_id=1, source_target_pairs={{0,4},{4,0},{8,12},{12,8},{16,20},{20,16},{24,28},{28,24},{1,5},{5... | collective-permute-start | bytes 3981320 | tf_op jit(solution)/shard_map/ppermute | solution.py:61
  106.4 29.4 %collective-permute-start.16 = (bf16[2,96,3456]{2,1,0:T(8,128)(2,1)S(1)}, bf16[2,96,3456]{2,1,0:T(8,128)(2,1)S(1)}, u32[]{:S(2)}, u32[]{:S(2)}) collective-permute-start(bf16[2,96,3456]{2,1,0:T(8,128)(2,1)S(1)} %pad_maximum_fusion.1.refs_0_), channel_id=1, source_target_pairs={{0,1},{1,0},{2,3},{3,2},{4,5},{5,4},{6,7},{7,6},{8,9},{9,8},{10,11... | collective-permute-start | bytes 3981320 | tf_op jit(solution)/shard_map/ppermute | solution.py:61
  106.4 26.0 %collective-permute-start.15 = (bf16[256,2304]{1,0:T(8,128)(2,1)S(1)}, bf16[256,2304]{1,0:T(8,128)(2,1)S(1)}, u32[]{:S(2)}, u32[]{:S(2)}) collective-permute-start(bf16[256,2304]{1,0:T(8,128)(2,1)S(1)} %get-tuple-element.184.refs_0_), channel_id=1, source_target_pairs={{0,1},{1,0},{2,3},{3,2},{4,5},{5,4},{6,7},{7,6},{8,9},{9,8},{10,11... | collective-permute-start | bytes 3538952 | tf_op jit(solution)/shard_map/ppermute | solution.py:61
  106.9 27.9 %collective-permute-start.14 = (bf16[256,2304]{1,0:T(8,128)(2,1)S(1)}, bf16[256,2304]{1,0:T(8,128)(2,1)S(1)}, u32[]{:S(2)}, u32[]{:S(2)}) collective-permute-start(bf16[256,2304]{1,0:T(8,128)(2,1)S(1)} %get-tuple-element.183), channel_id=1, source_target_pairs={{0,2},{1,3},{2,0},{3,1},{4,6},{5,7},{6,4},{7,5},{8,10},{9,11},{10,... | collective-permute-start | bytes 3538952 | tf_op jit(solution)/shard_map/ppermute | solution.py:61
  137.2 30.0 %collective-permute-start.18 = (bf16[2,128,768]{2,1,0:T(8,128)(2,1)S(1)}, bf16[2,128,768]{2,1,0:T(8,128)(2,1)S(1)}, u32[]{:S(2)}, u32[]{:S(2)}) collective-permute-start(bf16[2,128,768]{2,1,0:T(8,128)(2,1)S(1)} %slice.142), channel_id=1, source_target_pairs={{0,2},{1,3},{2,0},{3,1},{4,6},{5,7},{6,4},{7,5},{8,10},{9,11},{10,... | collective-permute-start | bytes 1179656 | tf_op jit(solution)/shard_map/ppermute | solution.py:61
  137.8 39.5 %collective-permute-start.21 = (bf16[2,96,3456]{2,1,0:T(8,128)(2,1)}, bf16[2,96,3456]{2,1,0:T(8,128)(2,1)}, u32[]{:S(2)}, u32[]{:S(2)}) collective-permute-start(bf16[2,96,3456]{2,1,0:T(8,128)(2,1)} %collective-permute-done.12.refs_1_), channel_id=1, source_target_pairs={{0,4},{4,0},{8,12},{12,8},{16,20},{20,16},{24,28},{28,24},{1,5},{5... | collective-permute-start | bytes 3981320 | tf_op jit(solution)/shard_map/ppermute | solution.py:61
  139.2 38.0 %collective-permute-start.22 = (bf16[2,96,3456]{2,1,0:T(8,128)(2,1)}, bf16[2,96,3456]{2,1,0:T(8,128)(2,1)}, u32[]{:S(2)}, u32[]{:S(2)}) collective-permute-start(bf16[2,96,3456]{2,1,0:T(8,128)(2,1)} %collective-permute-done.12.refs_1_), channel_id=1, source_target_pairs={{0,1},{1,0},{2,3},{3,2},{4,5},{5,4},{6,7},{7,6},{8,9},{9,8},{10,11... | collective-permute-start | bytes 3981320 | tf_op jit(solution)/shard_map/ppermute | solution.py:61
  139.3 38.0 %collective-permute-start.23 = (bf16[2,96,3456]{2,1,0:T(8,128)(2,1)}, bf16[2,96,3456]{2,1,0:T(8,128)(2,1)}, u32[]{:S(2)}, u32[]{:S(2)}) collective-permute-start(bf16[2,96,3456]{2,1,0:T(8,128)(2,1)} %collective-permute-done.13.refs_2_), channel_id=1, source_target_pairs={{0,1},{1,0},{2,3},{3,2},{4,5},{5,4},{6,7},{7,6},{8,9},{9,8},{10,11... | collective-permute-start | bytes 3981320 | tf_op jit(solution)/shard_map/ppermute | solution.py:61
  237.5 18.2 %collective-permute-start.25 = (bf16[768,1920]{1,0:T(8,128)(2,1)}, bf16[768,1920]{1,0:T(8,128)(2,1)}, u32[]{:S(2)}, u32[]{:S(2)}) collective-permute-start(bf16[768,1920]{1,0:T(8,128)(2,1)} %get-tuple-element.205), channel_id=1, source_target_pairs={{0,1},{1,0},{2,3},{3,2},{4,5},{5,4},{6,7},{7,6},{8,9},{9,8},{10,11... | collective-permute-start | bytes 8847368 | tf_op jit(solution)/shard_map/ppermute | solution.py:61
  253.9 57.0 %collective-permute-start.29 = (bf16[2,128,768]{2,1,0:T(8,128)(2,1)}, bf16[2,128,768]{2,1,0:T(8,128)(2,1)}, u32[]{:S(2)}, u32[]{:S(2)}) collective-permute-start(bf16[2,128,768]{2,1,0:T(8,128)(2,1)} %slice_bitcast_fusion.4), channel_id=1, source_target_pairs={{0,2},{1,3},{2,0},{3,1},{4,6},{5,7},{6,4},{7,5},{8,10},{9,11},{10,... | collective-permute-start | bytes 1179656 | tf_op jit(solution)/shard_map/ppermute | solution.py:61
  263.7 41.4 %collective-permute-start.31 = (bf16[2,2,192,768]{3,2,0,1:T(8,128)(2,1)}, bf16[2,2,192,768]{3,2,0,1:T(8,128)(2,1)}, u32[]{:S(2)}, u32[]{:S(2)}) collective-permute-start(bf16[2,2,192,768]{3,2,0,1:T(8,128)(2,1)} %bitcast.152), channel_id=1, source_target_pairs={{0,8},{4,12},{8,0},{12,4},{16,24},{20,28},{24,16},{28,20},{1,9},{5... | collective-permute-start | bytes 3538952 | tf_op jit(solution)/shard_map/ppermute | solution.py:61
  263.7 44.1 %collective-permute-start.30 = (bf16[2,2,96,1920]{3,2,0,1:T(8,128)(2,1)}, bf16[2,2,96,1920]{3,2,0,1:T(8,128)(2,1)}, u32[]{:S(2)}, u32[]{:S(2)}) collective-permute-start(bf16[2,2,96,1920]{3,2,0,1:T(8,128)(2,1)} %bitcast.151), channel_id=1, source_target_pairs={{0,4},{4,0},{8,12},{12,8},{16,20},{20,16},{24,28},{28,24},{1,5},{5... | collective-permute-start | bytes 4423688 | tf_op jit(solution)/shard_map/ppermute | solution.py:61
  318.1 28.4 %collective-permute-start.34 = (bf16[2304,256]{1,0:T(8,128)(2,1)}, bf16[2304,256]{1,0:T(8,128)(2,1)S(1)}, u32[]{:S(2)}, u32[]{:S(2)}) collective-permute-start(bf16[2304,256]{1,0:T(8,128)(2,1)} %get-tuple-element.366), channel_id=1, source_target_pairs={{0,2},{1,3},{2,0},{3,1},{4,6},{5,7},{6,4},{7,5},{8,10},{9,11},{10,... | collective-permute-start | bytes 3538952 | tf_op jit(solution)/shard_map/ppermute | solution.py:61
  319.6 26.1 %collective-permute-start.35 = (bf16[2,96,1920]{2,1,0:T(8,128)(2,1)}, bf16[2,96,1920]{2,1,0:T(8,128)(2,1)}, u32[]{:S(2)}, u32[]{:S(2)}) collective-permute-start(bf16[2,96,1920]{2,1,0:T(8,128)(2,1)} %get-tuple-element.376), channel_id=1, source_target_pairs={{0,8},{4,12},{8,0},{12,4},{16,24},{20,28},{24,16},{28,20},{1,9},{5... | collective-permute-start | bytes 2211848 | tf_op jit(solution)/shard_map/ppermute | solution.py:61
  321.5 24.3 %collective-permute-start.36 = (bf16[2,192,768]{2,1,0:T(8,128)(2,1)}, bf16[2,192,768]{2,1,0:T(8,128)(2,1)}, u32[]{:S(2)}, u32[]{:S(2)}) collective-permute-start(bf16[2,192,768]{2,1,0:T(8,128)(2,1)} %get-tuple-element.380), channel_id=1, source_target_pairs={{0,4},{4,0},{8,12},{12,8},{16,20},{20,16},{24,28},{28,24},{1,5},{5... | collective-permute-start | bytes 1769480 | tf_op jit(solution)/shard_map/ppermute | solution.py:61
  359.7 25.3 %collective-permute-start.40 = (bf16[192,768]{1,0:T(8,128)(2,1)}, bf16[192,768]{1,0:T(8,128)(2,1)}, u32[]{:S(2)}, u32[]{:S(2)}) collective-permute-start(bf16[192,768]{1,0:T(8,128)(2,1)} %dynamic-slice_bitcast_fusion.6), channel_id=1, source_target_pairs={{0,16},{4,20},{8,24},{12,28},{16,0},{20,4},{24,8},{28,12},{1,17},{... | collective-permute-start | bytes 884744 | tf_op jit(solution)/shard_map/ppermute | solution.py:61
  359.9 36.8 %collective-permute-start.38 = (bf16[2304,256]{1,0:T(8,128)(2,1)}, bf16[2304,256]{1,0:T(8,128)(2,1)}, u32[]{:S(2)}, u32[]{:S(2)}) collective-permute-start(bf16[2304,256]{1,0:T(8,128)(2,1)} %get-tuple-element.364), channel_id=1, source_target_pairs={{0,2},{1,3},{2,0},{3,1},{4,6},{5,7},{6,4},{7,5},{8,10},{9,11},{10,... | collective-permute-start | bytes 3538952 | tf_op jit(solution)/shard_map/ppermute | solution.py:61
  372.2 19.9 %collective-permute-start.39 = (bf16[96,1920]{1,0:T(8,128)(2,1)}, bf16[96,1920]{1,0:T(8,128)(2,1)}, u32[]{:S(2)}, u32[]{:S(2)}) collective-permute-start(bf16[96,1920]{1,0:T(8,128)(2,1)} %dynamic-slice_bitcast_fusion.4), channel_id=1, source_target_pairs={{0,16},{4,20},{8,24},{12,28},{16,0},{20,4},{24,8},{28,12},{1,17},{... | collective-permute-start | bytes 1105928 | tf_op jit(solution)/shard_map/ppermute | solution.py:61
  417.7 18.3 %collective-permute-start.49 = (bf16[2,2,96,768]{3,2,0,1:T(8,128)(2,1)S(1)}, bf16[2,2,96,768]{3,2,0,1:T(8,128)(2,1)S(1)}, u32[]{:S(2)}, u32[]{:S(2)}) collective-permute-start(bf16[2,2,96,768]{3,2,0,1:T(8,128)(2,1)S(1)} %bitcast.182), channel_id=1, source_target_pairs={{0,4},{4,0},{8,12},{12,8},{16,20},{20,16},{24,28},{28,24},{1,5},{5... | collective-permute-start | bytes 1769480 | tf_op jit(solution)/shard_map/ppermute | solution.py:61
  434.0 24.9 %collective-permute-start.54 = (f32[16,128]{1,0:T(8,128)S(1)}, f32[16,128]{1,0:T(8,128)S(1)}, u32[]{:S(2)}, u32[]{:S(2)}) collective-permute-start(f32[16,128]{1,0:T(8,128)S(1)} %fusion.35), channel_id=1, source_target_pairs={{0,2},{1,3},{2,0},{3,1},{4,6},{5,7},{6,4},{7,5},{8,10},{9,11},{10,... | collective-permute-start | bytes 24584 | tf_op jit(solution)/shard_map/ppermute | solution.py:61
  (89 other events, 859.2 us)
